TPU v7x, 512 devices: a whole 4x8x8 slice. The times are simulated.
512 devices in a mesh: dp: 64 (over z, y_lo, x), mp: 8 (over y_hi, core).
Axes of the slice: x: 4, y: 8 (y_hi: 4, y_lo: 2; y = y_hi * 2 + y_lo), z: 8, core: 2. Of those that a mesh axis runs over, the one named last changes fastest.
Arguments:
- activations: bfloat16 [49152, 4096], P('dp', 'mp'), may hold values from -16 to 16
- query_rows: bfloat16 [49152, 4096], P('dp', 'mp'), may hold values from -84 to 84
- key_rows: bfloat16 [49152, 1024], P('dp', 'mp'), may hold values from -5 to 5
- true_cotangent: bfloat16 [49152, 4096], P('dp', 'mp'), may hold values from -6 to 6
- sample_cotangent: bfloat16 [49152, 4096], P('dp', 'mp'), may hold values from -6 to 6
- master: float32 [4096, 1024], P('dp', 'mp'), may hold values from -0.09375 to 0.09375
- moment: float32 [4096, 1024], P('dp', 'mp'), may hold values from -6 to 6
- curvature: float32 [4096, 1024], P('dp', 'mp'), may hold values from 5 to 50
Outputs:
- master_next: float32 [4096, 1024], P('dp', 'mp')
- moment_next: float32 [4096, 1024], P('dp', 'mp')
- curvature_next: float32 [4096, 1024], P('dp', 'mp')
- weights_next: bfloat16 [4096, 1024], P(None, 'mp')
All inputs are finite; a program needn't handle non-finite values.
Results may differ from a plain program's by a relative error of at most 0.012.
Values may be sent and summed in bfloat16 or wider, within the bound.
No kernel may reach another device: no remote copies, remote signals or barrier semaphores. Data moves between devices by JAX's collectives and lax.ppermute only.
A program may use at most 64 MiB of HBM per device.

v0:
```python
import jax
import jax.numpy as jnp
from jax import lax
from jax.sharding import PartitionSpec as P

HQ = 32
KVH = 8
HD = 128


momentum_decay = 0.965
curvature_decay = 0.99
clip_scale = 0.04
learn_rate = 0.0006
weight_decay = 0.1


def shards(
    activations, query_rows, key_rows, true_cotangent, sample_cotangent, master, moment, curvature
):
    tok_count = query_rows.shape[0]
    kv_local = key_rows.shape[1] // HD
    group_size = HQ // KVH
    query_heads = query_rows.reshape(tok_count, kv_local, group_size, HD)
    key_heads = key_rows.reshape(tok_count, kv_local, HD)
    scores = jnp.einsum(
        "qkgd,skd->kgqs", query_heads, key_heads, preferred_element_type=jnp.float32
    ) * HD ** (-0.5)
    causal = lax.broadcasted_iota(jnp.int32, (tok_count, tok_count), 0) >= lax.broadcasted_iota(
        jnp.int32, (tok_count, tok_count), 1
    )
    masked = jnp.where(causal, scores, -jnp.inf)
    highest = jnp.max(masked, axis=-1, keepdims=True)
    powers = jnp.exp(masked - highest)
    attention = (powers / jnp.sum(powers, axis=-1, keepdims=True)).astype(jnp.bfloat16)
    cotangents = jnp.stack((true_cotangent, sample_cotangent)).reshape(
        2, tok_count, kv_local, group_size, HD
    )
    value_grads = jnp.einsum(
        "kgqs,cqkgd->sckd", attention, cotangents, preferred_element_type=jnp.float32
    )
    value_grads = value_grads.astype(jnp.bfloat16).reshape(tok_count, 2 * kv_local * HD)
    contract = (((0,), (0,)), ((), ()))
    width_local = kv_local * HD
    gathered = lax.all_gather(activations, "mp", axis=1, tiled=True)
    summed = lax.psum_scatter(
        lax.dot_general(gathered, value_grads, contract, preferred_element_type=jnp.float32),
        "dp",
        scatter_dimension=0,
        tiled=True,
    )
    grad_true = summed[:, :width_local]
    grad_sample = summed[:, width_local:]
    moment_next = momentum_decay * moment + (1.0 - momentum_decay) * grad_true
    curvature_next = (
        curvature_decay * curvature + (1.0 - curvature_decay) * grad_sample * grad_sample
    )
    ratio = jnp.clip(moment_next / (clip_scale * curvature_next), -1.0, 1.0)
    master_next = master * (1.0 - learn_rate * weight_decay) - learn_rate * ratio
    weights_next = lax.all_gather(master_next.astype(jnp.bfloat16), "dp", axis=0, tiled=True)
    return (master_next, moment_next, curvature_next, weights_next)


def solution(mesh):
    placed = (
        P("dp", "mp"),
        P("dp", "mp"),
        P("dp", "mp"),
        P("dp", "mp"),
        P("dp", "mp"),
        P("dp", "mp"),
        P("dp", "mp"),
        P("dp", "mp"),
    )
    return jax.shard_map(
        shards,
        mesh=mesh,
        in_specs=placed,
        out_specs=(P("dp", "mp"), P("dp", "mp"), P("dp", "mp"), P(None, "mp")),
        check_vma=False,
    )
```

profile of v0, /device:TPU:16, one launch (start us, length us, event | category | flops | bytes accessed | tf_op | source)
XLA Modules:
  0.0 730.7 jit_solution(698033668703633222)
XLA Ops:
  7.2 0.0 copy-start
  7.2 0.0 all-gather.3.cloned.1.call-start
  7.2 0.7 all-gather.3.cloned.1.call-update
  7.9 0.0 reduce-scatter.4.cloned.1.call-start
  8.0 1.4 copy.34
  9.4 1.4 copy.35
  10.8 0.2 iota_compare_fusion
  11.0 0.0 copy-done
  11.0 2.6 fusion.1
  13.6 2.0 fusion
  15.6 3.2 fusion.9
  18.8 68.6 %all-gather.3.cloned.1.call-done = bf16[768,4096]{1,0:T(8,128)(2,1)} async-done(((bf16[768,512]{1,0:T(8,128)(2,1)}), bf16[768,4096]{1,0:T(8,128)(2,1)}) %all-gather.3.cloned.1.call-update) | async-done | bytes 6291472 | tf_op jit(solution)/shard_map/all_gather | solution.py:45
  87.4 0.0 copy-start.1
  87.4 0.0 copy-start.2
  87.4 0.0 copy-start.3
  87.4 6.6 convolution_bitcast_fusion
  94.0 5.6 copy.43
  99.6 0.0 reduce-scatter.4.cloned.1.call-update
  99.6 0.0 all-gather.5.cloned.1.call-start
  99.7 324.1 %reduce-scatter.4.cloned.1.call-done = f32[64,256]{1,0:T(8,128)} async-done(((f32[4096,256]{1,0:T(8,128)}), f32[64,256]{1,0:T(8,128)}) %reduce-scatter.4.cloned.1.call-update) | async-done | bytes 65552 | tf_op jit(solution)/shard_map/reduce_scatter | solution.py:46
  423.8 0.0 copy-done.1
  423.8 0.0 copy-done.2
  423.8 0.0 copy-done.3
  423.8 1.4 fusion.21
  425.2 0.0 all-gather.5.cloned.1.call-update
  425.3 296.6 %all-gather.5.cloned.1.call-done = bf16[4096,128]{1,0:T(8,128)(2,1)} async-done(((bf16[64,128]{1,0:T(8,128)(2,1)}), bf16[4096,128]{1,0:T(8,128)(2,1)}) %all-gather.5.cloned.1.call-update) | async-done | bytes 1048592 | tf_op jit(solution)/shard_map/all_gather | solution.py:60
  721.9 2.3 copy.53
Async XLA Ops:
  7.2 3.8 copy-start
  7.2 80.2 %all-gather.3.cloned.1.call-start = ((), (), s32[]{:S(2)}) async-start(), calls=%async_computation.1 | async-start | bytes 7077888 | tf_op jit(solution)/shard_map/all_gather | solution.py:45
  7.9 415.9 %reduce-scatter.4.cloned.1.call-start = ((), (), s32[]{:S(2)}) async-start(), calls=%async_computation.3 | async-start | bytes 4259840 | tf_op jit(solution)/shard_map/reduce_scatter | solution.py:46
  87.4 336.4 %copy-start.1 = (f32[64,128]{1,0:T(8,128)S(1)}, f32[64,128]{1,0:T(8,128)}, u32[]{:S(2)}) copy-start(f32[64,128]{1,0:T(8,128)} %param.13) | copy-start | bytes 98308
  87.4 336.4 %copy-start.2 = (f32[64,128]{1,0:T(8,128)S(1)}, f32[64,128]{1,0:T(8,128)}, u32[]{:S(2)}) copy-start(f32[64,128]{1,0:T(8,128)} %param.15) | copy-start | bytes 98308
  87.4 336.4 %copy-start.3 = (f32[64,128]{1,0:T(8,128)S(1)}, f32[64,128]{1,0:T(8,128)}, u32[]{:S(2)}) copy-start(f32[64,128]{1,0:T(8,128)} %param.14) | copy-start | bytes 98308
  99.6 622.3 %all-gather.5.cloned.1.call-start = ((), (), s32[]{:S(2)}) async-start(), calls=%async_computation.2 | async-start | bytes 1064960 | tf_op jit(solution)/shard_map/all_gather | solution.py:60
Sparse Core Ops, SparseCore 0:
  10.1 77.2 all-gather.2
  99.8 323.9 reduce-scatter.3
  426.7 295.1 all-gather.4
where the time goes:
time: 731 us
  waiting for transfers between devices  690 us (94%)
  between operations  13.8 us (2%)
  matrix products  12.4 us (2%)
  local copies, waits for them, and re-layouts  10.7 us (1%)
    reduce_scatter x1, waiting for transfers between devices, shards(): lax.psum_scatter(lax.dot_general(gathered, value_grads, contract, preferr...  324 us
    all_gather x1, waiting for transfers between devices, shards(): lax.all_gather(master_next.astype(jnp.bfloat16), 'dp', axis=0, tiled=True)  297 us
    all_gather x1, waiting for transfers between devices, shards(): gathered = lax.all_gather(activations, 'mp', axis=1, tiled=True)  68.6 us
  transfers between devices with their start and end apart: 3, of which 3 were waited for; matrix products, arithmetic and copies ran while one was open for 1% of the time, Pallas kernels for 0%

commit v1 on v0

v1 whole, which is shorter than its diff:
```python
import jax
import jax.numpy as jnp
from jax import lax
from jax.sharding import Mesh, PartitionSpec as P

HQ = 32
KVH = 8
HD = 128

AXES = ("zh", "zl", "yl", "x", "yh", "c")
SIZES = (4, 2, 2, 4, 4, 2)
NEAR = ("zl", "yl", "x")

momentum_decay = 0.965
curvature_decay = 0.99
clip_scale = 0.04
learn_rate = 0.0006
weight_decay = 0.1


def shift(v, axis, size, step):
    return lax.ppermute(v, axis, [(i, (i + step) % size) for i in range(size)])


def attention_grads(query_rows, key_rows, true_cotangent, sample_cotangent):
    tok_count = query_rows.shape[0]
    kv_local = key_rows.shape[1] // HD
    group_size = HQ // KVH
    query_heads = query_rows.reshape(tok_count, kv_local, group_size, HD)
    key_heads = key_rows.reshape(tok_count, kv_local, HD)
    scores = jnp.einsum(
        "qkgd,skd->kgqs", query_heads, key_heads, preferred_element_type=jnp.float32
    ) * HD ** (-0.5)
    causal = lax.broadcasted_iota(jnp.int32, (tok_count, tok_count), 0) >= lax.broadcasted_iota(
        jnp.int32, (tok_count, tok_count), 1
    )
    masked = jnp.where(causal, scores, -jnp.inf)
    highest = jnp.max(masked, axis=-1, keepdims=True)
    powers = jnp.exp(masked - highest)
    attention = (powers / jnp.sum(powers, axis=-1, keepdims=True)).astype(jnp.bfloat16)
    cotangents = jnp.stack((true_cotangent, sample_cotangent)).reshape(
        2, tok_count, kv_local, group_size, HD
    )
    value_grads = jnp.einsum(
        "kgqs,cqkgd->sckd", attention, cotangents, preferred_element_type=jnp.float32
    )
    return value_grads.astype(jnp.bfloat16).reshape(tok_count, 2 * kv_local * HD)


def shards(
    activations, query_rows, key_rows, true_cotangent, sample_cotangent, master, moment, curvature
):
    zh, yh, core = lax.axis_index("zh"), lax.axis_index("yh"), lax.axis_index("c")
    rows, width = master.shape
    state = jnp.concatenate((master, moment, curvature), axis=0)
    states = lax.all_gather(state, ("zh", "zl"), axis=0).reshape(4, 2, 3, rows, width)
    states = lax.dynamic_index_in_dim(states, lax.axis_index("zl"), 1, keepdims=False)
    sibling = shift(activations, "c", 2, 1)
    features = jnp.concatenate(
        (
            jnp.where(core == 0, activations, sibling),
            jnp.where(core == 0, sibling, activations),
        ),
        axis=1,
    )
    own = attention_grads(query_rows, key_rows, true_cotangent, sample_cotangent)
    half = own.shape[0] // 2
    below = shift(own, "yh", 4, 1)
    above = shift(own, "yh", 4, -1)
    far_first = shift(below[:half], "yh", 4, 1)
    far_last = shift(above[half:], "yh", 4, -1)
    far = jnp.concatenate((far_first, far_last), axis=0)
    ring = jnp.stack((own, above, far, below))
    contract = (((0,), (0,)), ((), ()))
    part = jnp.stack(
        [
            lax.dot_general(features, ring[i], contract, preferred_element_type=jnp.float32).astype(
                jnp.bfloat16
            )
            for i in range(4)
        ]
    )
    part = jnp.roll(part, yh, axis=0)
    part = part.reshape(4, 16, rows, 2 * width).transpose(1, 0, 2, 3)
    part = lax.all_to_all(part, NEAR, 0, 0, tiled=True)
    part = jnp.sum(part.astype(jnp.float32), axis=0).astype(jnp.bfloat16)
    part = jnp.broadcast_to(part[None], (4, 4, rows, 2 * width)).reshape(16, rows, 2 * width)
    part = lax.all_to_all(part, ("zh", "yh"), 0, 0, tiled=True)
    summed = jnp.sum(part.reshape(4, 4, rows, 2 * width).astype(jnp.float32), axis=0)
    grad_true = summed[..., :width]
    grad_sample = summed[..., width:]
    moment_next = momentum_decay * states[:, 1] + (1.0 - momentum_decay) * grad_true
    curvature_next = (
        curvature_decay * states[:, 2] + (1.0 - curvature_decay) * grad_sample * grad_sample
    )
    ratio = jnp.clip(moment_next / (clip_scale * curvature_next), -1.0, 1.0)
    master_next = states[:, 0] * (1.0 - learn_rate * weight_decay) - learn_rate * ratio
    weights = master_next.astype(jnp.bfloat16)
    weights = jnp.broadcast_to(weights[None], (16, 4, rows, width))
    weights = lax.all_to_all(weights, NEAR, 0, 0, tiled=True)
    weights_next = weights.transpose(1, 0, 2, 3).reshape(64 * rows, width)
    mine = lambda v: lax.dynamic_index_in_dim(v, zh, 0, keepdims=False)
    return (mine(master_next), mine(moment_next), mine(curvature_next), weights_next)


def solution(mesh):
    fine = Mesh(mesh.devices.reshape(SIZES), AXES)
    dp, mp = AXES[:4], AXES[4:]
    placed = (P(dp, mp),) * 8
    return jax.shard_map(
        shards,
        mesh=fine,
        in_specs=placed,
        out_specs=(P(dp, mp), P(dp, mp), P(dp, mp), P(None, mp)),
        check_vma=False,
    )
```

time: 731 us -> 161 us (0.22)
  waiting for transfers between devices: 690 us -> 32.5 us
  blocking collectives: 0 us -> 70.6 us
  starting transfers between devices: 0.12 us -> 35.9 us
  between operations: 13.8 us -> 0.93 us
    all_gather x2 -> x0, waiting for transfers between devices: 365 us -> none  [the longest x1 297 us: shards(): lax.all_gather(master_next.astype(jnp.bfloat16), 'dp', axis=0, tiled=True)]
    reduce_scatter x1 -> x0, waiting for transfers between devices: 324 us -> none  [shards(): lax.psum_scatter(lax.dot_general(gathered, value_grads, contract, preferr...]
    all_to_all x0 -> x1, blocking collectives: none -> 37.2 us  [shards(): part = lax.all_to_all(part, NEAR, 0, 0, tiled=True)]
    all_gather x0 -> x1, blocking collectives: none -> 33.4 us  [shards(): lax.all_gather(state, ('zh', 'zl'), axis=0).reshape(4, 2, 3, rows, width)]
    ppermute x0 -> x5, waiting for transfers between devices: none -> 21.1 us  [shift(): return lax.ppermute(v, axis, [(i, (i + step) % size) for i in range(size)])]
    ppermute x0 -> x5, starting transfers between devices: none -> 19.6 us  [shift(): return lax.ppermute(v, axis, [(i, (i + step) % size) for i in range(size)])]
    all_to_all x0 -> x2, starting transfers between devices: none -> 16.3 us  [the longest x1 11.8 us: shards(): part = lax.all_to_all(part, ('zh', 'yh'), 0, 0, tiled=True)]
    all_to_all x0 -> x2, waiting for transfers between devices: none -> 11.4 us  [the longest x1 11.4 us: shards(): weights = lax.all_to_all(weights, NEAR, 0, 0, tiled=True)]
  transfers between devices with their start and end apart: 3 -> 7, of which waited for: 3 -> 4; matrix products, arithmetic and copies ran while one was open for 1% -> 9% of each run, Pallas kernels for 0% -> 0%
where the time goes in v1:
time: 161 us; the launch traced here: 160 us
  blocking collectives  70.6 us (44%)
  starting transfers between devices  35.9 us (22%)
  waiting for transfers between devices  32.5 us (20%)
  matrix products  8.29 us (5%)
  local copies, waits for them, and re-layouts  7.82 us (5%)
  other arithmetic  4.25 us (3%)
    all_to_all x1, blocking collectives, shards(): part = lax.all_to_all(part, NEAR, 0, 0, tiled=True)  37.2 us
    all_gather x1, blocking collectives, shards(): lax.all_gather(state, ('zh', 'zl'), axis=0).reshape(4, 2, 3, rows, width)  33.4 us
    ppermute x5, waiting for transfers between devices, shift(): return lax.ppermute(v, axis, [(i, (i + step) % size) for i in range(size)])  21.1 us
    ppermute x5, starting transfers between devices, shift(): return lax.ppermute(v, axis, [(i, (i + step) % size) for i in range(size)])  19.6 us
    all_to_all x1, starting transfers between devices, shards(): part = lax.all_to_all(part, ('zh', 'yh'), 0, 0, tiled=True)  11.8 us
    all_to_all x1, waiting for transfers between devices, shards(): weights = lax.all_to_all(weights, NEAR, 0, 0, tiled=True)  11.4 us
    all_to_all x1, starting transfers between devices, shards(): weights = lax.all_to_all(weights, NEAR, 0, 0, tiled=True)  4.48 us
  transfers between devices with their start and end apart: 7, of which 4 were waited for; matrix products, arithmetic and copies ran while one was open for 9% of the time, Pallas kernels for 0%

profile of v1, /device:TPU:16, one launch (start us, length us, event | category | flops | bytes accessed | tf_op | source)
XLA Modules:
  0.0 160.2 jit_solution(9137369927614581268)
XLA Ops:
  0.6 2.1 %collective-permute-start = (bf16[768,512]{1,0:T(8,128)(2,1)}, bf16[768,512]{1,0:T(8,128)(2,1)}, u32[]{:S(2)}, u32[]{:S(2)}) collective-permute-start(bf16[768,512]{1,0:T(8,128)(2,1)} %param.8), channel_id=1, source_target_pairs={{0,1},{1,0},{2,3},{3,2},{4,5},{5,4},{6,7},{7,6},{8,9},{9,8},{10,11... | collective-permute-start | bytes 2359304 | tf_op jit(solution)/shard_map/ppermute | solution.py:22
  2.7 0.2 iota_compare_fusion
  2.9 1.4 copy.30
  4.3 1.4 copy.31
  5.7 2.6 %fusion.1 = (f32[4,768]{1,0:T(4,128)S(1)}, f32[768,768,4]{1,0,2:T(8,128)S(1)}) fusion(pred[768,768]{0,1:T(8,128)(4,1)S(1)} %iota_compare_fusion, bf16[768,128]{1,0:T(8,128)(2,1)} %param.10, bf16[768,512]{1,0:T(8,128)(2,1)S(1)} %copy-done), kind=kOutput, calls=%fused_computation.4 | convolution fusion | flops 611054592 | bytes 11022336 | tf_op jit(solution)/shard_map/qkgd,skd->kgqs/dot_general | solution.py:31
  8.3 2.0 %fusion = f32[4,768]{1,0:T(4,128)S(1)} fusion(f32[768,768,4]{1,0,2:T(8,128)S(1)} %get-tuple-element.11, f32[4,768]{1,0:T(4,128)S(1)} %get-tuple-element.10, pred[768,768]{0,1:T(8,128)(4,1)S(1)} %iota_compare_fusion), kind=kLoop, calls=%fused_computation.3 | loop fusion | flops 9434112 | bytes 10051584 | tf_op jit(solution)/shard_map/reduce_sum | solution.py:40
  10.4 3.2 %fusion.9 = bf16[2,128,768]{2,1,0:T(8,128)(2,1)S(1)} fusion(f32[4,768]{1,0:T(4,128)S(1)} %fusion, f32[4,768]{1,0:T(4,128)S(1)} %get-tuple-element.10, f32[768,768,4]{1,0,2:T(8,128)S(1)} %get-tuple-element.11, pred[768,768]{0,1:T(8,128)(4,1)S(1)} %iota_compare_fusion, bf16[1,768,1,4,128]{1,4,3,0,2:T(8,128)(2,1)S(1)} %bitcast.108, ...), kind=kOutput, calls=%fused_computation.17 | convolution fusion | flops 1220739072 | bytes 12017664 | tf_op jit(solution)/shard_map/kgqs,cqkgd->sckd/dot_general | solution.py:44
  13.6 5.7 %collective-permute-start.2 = (bf16[768,256]{0,1:T(8,128)(2,1)S(1)}, bf16[768,256]{0,1:T(8,128)(2,1)S(1)}, u32[]{:S(2)}, u32[]{:S(2)}) collective-permute-start(bf16[768,256]{0,1:T(8,128)(2,1)S(1)} %bitcast.109), channel_id=1, source_target_pairs={{0,2},{2,4},{4,6},{6,0},{1,3},{3,5},{5,7},{7,1},{8,10},{10,12},{12... | collective-permute-start | bytes 1179656 | tf_op jit(solution)/shard_map/ppermute | solution.py:22
  19.3 3.8 %collective-permute-start.1 = (bf16[768,256]{0,1:T(8,128)(2,1)S(1)}, bf16[768,256]{0,1:T(8,128)(2,1)S(1)}, u32[]{:S(2)}, u32[]{:S(2)}) collective-permute-start(bf16[768,256]{0,1:T(8,128)(2,1)S(1)} %bitcast.110), channel_id=1, source_target_pairs={{0,6},{2,0},{4,2},{6,4},{1,7},{3,1},{5,3},{7,5},{8,14},{10,8},{12,... | collective-permute-start | bytes 1179656 | tf_op jit(solution)/shard_map/ppermute | solution.py:22
  23.1 14.4 %collective-permute-done.2 = bf16[768,256]{0,1:T(8,128)(2,1)S(1)} collective-permute-done((bf16[768,256]{0,1:T(8,128)(2,1)S(1)}, bf16[768,256]{0,1:T(8,128)(2,1)S(1)}, u32[]{:S(2)}, u32[]{:S(2)}) %collective-permute-start.2) | collective-permute-done | bytes 393248 | tf_op jit(solution)/shard_map/ppermute | solution.py:22
  37.6 4.5 %collective-permute-start.3 = (bf16[384,256]{0,1:T(8,128)(2,1)S(1)}, bf16[384,256]{0,1:T(8,128)(2,1)S(1)}, u32[]{:S(2)}, u32[]{:S(2)}) collective-permute-start(bf16[384,256]{0,1:T(8,128)(2,1)S(1)} %slice.30), channel_id=1, source_target_pairs={{0,2},{2,4},{4,6},{6,0},{1,3},{3,5},{5,7},{7,1},{8,10},{10,12},{12... | collective-permute-start | bytes 589832 | tf_op jit(solution)/shard_map/ppermute | solution.py:22
  42.1 3.5 %collective-permute-start.4 = (bf16[384,256]{0,1:T(8,128)(2,1)S(1)}, bf16[384,256]{0,1:T(8,128)(2,1)S(1)}, u32[]{:S(2)}, u32[]{:S(2)}) collective-permute-start(bf16[384,256]{0,1:T(8,128)(2,1)S(1)} %slice.31), channel_id=1, source_target_pairs={{0,6},{2,0},{4,2},{6,4},{1,7},{3,1},{5,3},{7,5},{8,14},{10,8},{12,... | collective-permute-start | bytes 589832 | tf_op jit(solution)/shard_map/ppermute | solution.py:22
  45.6 1.5 broadcast_select_fusion.1
  47.1 0.6 constant_dynamic-update-slice_fusion.7
  47.7 0.6 constant_dynamic-update-slice_fusion.6
  48.4 1.1 collective-permute-done.3
  49.5 5.6 %collective-permute-done.4 = bf16[384,256]{0,1:T(8,128)(2,1)S(1)} collective-permute-done((bf16[384,256]{0,1:T(8,128)(2,1)S(1)}, bf16[384,256]{0,1:T(8,128)(2,1)S(1)}, u32[]{:S(2)}, u32[]{:S(2)}) %collective-permute-start.4) | collective-permute-done | bytes 196640 | tf_op jit(solution)/shard_map/ppermute | solution.py:22
  55.0 0.6 constant_dynamic-update-slice_fusion.5
  55.7 0.6 constant_dynamic-update-slice_fusion.4
  56.5 0.1 constant_dynamic-slice_fusion
  56.6 0.2 copy.34
  56.9 37.2 %all_to_all.15 = bf16[16,4,64,256]{3,2,1,0:T(8,128)(2,1)S(1)} all-to-all(bf16[16,4,64,256]{3,2,1,0:T(8,128)(2,1)S(1)} %copy.34), channel_id=1, replica_groups=mesh['zh'=4,'zl'=2,'yl'=2,'x'=4,'yh'=4,'c'=2] {'zl','yl','x'}, dimensions={0} | all-to-all | bytes 4194304 | tf_op jit(solution)/shard_map/all_to_all | solution.py:85
  94.1 0.4 reduce_sum.31
  94.5 0.8 broadcast_in_dim.24
  95.4 11.8 %all-to-all-start.1 = ((bf16[16,64,256]{2,1,0:T(8,128)(2,1)}), bf16[16,64,256]{2,1,0:T(8,128)(2,1)S(1)}, u32[]{:S(2)}, u32[]{:S(2)}) async-start(bf16[16,64,256]{2,1,0:T(8,128)(2,1)} %bitcast.25), calls=%async_computation.1 | async-start | bytes 1048576 | tf_op jit(solution)/shard_map/all_to_all | solution.py:88
  107.2 33.4 %all-gather = f32[1536,128]{1,0:T(8,128)S(1)} all-gather(f32[192,128]{1,0:T(8,128)S(1)} %pad_maximum_fusion.1), channel_id=2, replica_groups=mesh['zh'=4,'zl'=2,'yl'=2,'x'=4,'yh'=4,'c'=2] {'zh','zl'}, dimensions={0}, use_global_device_ids=true | all-gather | bytes 884736 | tf_op jit(solution)/shard_map/all_gather | solution.py:56
  140.8 1.2 broadcast_in_dim.25
  142.0 4.5 %all-to-all-start.2 = ((bf16[16,4,64,128]{3,2,1,0:T(8,128)(2,1)}), bf16[16,4,64,128]{3,2,1,0:T(8,128)(2,1)S(1)}, u32[]{:S(2)}, u32[]{:S(2)}) async-start(bf16[16,4,64,128]{3,2,1,0:T(8,128)(2,1)} %broadcast_in_dim.25), calls=%async_computation.2 | async-start | bytes 2097152 | tf_op jit(solution)/shard_map/all_to_all | solution.py:100
  146.5 0.6 dynamic-slice_bitcast_fusion.2
  147.1 0.6 dynamic-slice_bitcast_fusion
  147.8 11.4 %all-to-all-done.2 = bf16[16,4,64,128]{3,2,1,0:T(8,128)(2,1)S(1)} async-done(((bf16[16,4,64,128]{3,2,1,0:T(8,128)(2,1)}), bf16[16,4,64,128]{3,2,1,0:T(8,128)(2,1)S(1)}, u32[]{:S(2)}, u32[]{:S(2)}) %all-to-all-start.2) | async-done | bytes 1048608 | tf_op jit(solution)/shard_map/all_to_all | solution.py:100
  159.1 1.1 copy.35
  (21 shorter events, 0.4 us)
Async XLA Ops:
  0.6 5.1 %copy-start = (bf16[768,512]{1,0:T(8,128)(2,1)S(1)}, bf16[768,512]{1,0:T(8,128)(2,1)}, u32[]{:S(2)}) copy-start(bf16[768,512]{1,0:T(8,128)(2,1)} %param.9) | copy-start | bytes 2359300
  0.6 45.0 %collective-permute-start = (bf16[768,512]{1,0:T(8,128)(2,1)}, bf16[768,512]{1,0:T(8,128)(2,1)}, u32[]{:S(2)}, u32[]{:S(2)}) collective-permute-start(bf16[768,512]{1,0:T(8,128)(2,1)} %param.8), channel_id=1, source_target_pairs={{0,1},{1,0},{2,3},{3,2},{4,5},{5,4},{6,7},{7,6},{8,9},{9,8},{10,11... | collective-permute-start | bytes 2359304 | tf_op jit(solution)/shard_map/ppermute | solution.py:22
  13.6 24.0 %collective-permute-start.2 = (bf16[768,256]{0,1:T(8,128)(2,1)S(1)}, bf16[768,256]{0,1:T(8,128)(2,1)S(1)}, u32[]{:S(2)}, u32[]{:S(2)}) collective-permute-start(bf16[768,256]{0,1:T(8,128)(2,1)S(1)} %bitcast.109), channel_id=1, source_target_pairs={{0,2},{2,4},{4,6},{6,0},{1,3},{3,5},{5,7},{7,1},{8,10},{10,12},{12... | collective-permute-start | bytes 1179656 | tf_op jit(solution)/shard_map/ppermute | solution.py:22
  19.3 22.8 %collective-permute-start.1 = (bf16[768,256]{0,1:T(8,128)(2,1)S(1)}, bf16[768,256]{0,1:T(8,128)(2,1)S(1)}, u32[]{:S(2)}, u32[]{:S(2)}) collective-permute-start(bf16[768,256]{0,1:T(8,128)(2,1)S(1)} %bitcast.110), channel_id=1, source_target_pairs={{0,6},{2,0},{4,2},{6,4},{1,7},{3,1},{5,3},{7,5},{8,14},{10,8},{12,... | collective-permute-start | bytes 1179656 | tf_op jit(solution)/shard_map/ppermute | solution.py:22
  37.6 11.9 %collective-permute-start.3 = (bf16[384,256]{0,1:T(8,128)(2,1)S(1)}, bf16[384,256]{0,1:T(8,128)(2,1)S(1)}, u32[]{:S(2)}, u32[]{:S(2)}) collective-permute-start(bf16[384,256]{0,1:T(8,128)(2,1)S(1)} %slice.30), channel_id=1, source_target_pairs={{0,2},{2,4},{4,6},{6,0},{1,3},{3,5},{5,7},{7,1},{8,10},{10,12},{12... | collective-permute-start | bytes 589832 | tf_op jit(solution)/shard_map/ppermute | solution.py:22
  42.1 12.9 %collective-permute-start.4 = (bf16[384,256]{0,1:T(8,128)(2,1)S(1)}, bf16[384,256]{0,1:T(8,128)(2,1)S(1)}, u32[]{:S(2)}, u32[]{:S(2)}) collective-permute-start(bf16[384,256]{0,1:T(8,128)(2,1)S(1)} %slice.31), channel_id=1, source_target_pairs={{0,6},{2,0},{4,2},{6,4},{1,7},{3,1},{5,3},{7,5},{8,14},{10,8},{12,... | collective-permute-start | bytes 589832 | tf_op jit(solution)/shard_map/ppermute | solution.py:22
  56.9 50.3 %copy-start.1 = (f32[64,128]{1,0:T(8,128)S(1)}, f32[64,128]{1,0:T(8,128)}, u32[]{:S(2)}) copy-start(f32[64,128]{1,0:T(8,128)} %param.15) | copy-start | bytes 98308
  56.9 50.3 %copy-start.2 = (f32[64,128]{1,0:T(8,128)S(1)}, f32[64,128]{1,0:T(8,128)}, u32[]{:S(2)}) copy-start(f32[64,128]{1,0:T(8,128)} %param.14) | copy-start | bytes 98308
  56.9 50.3 %copy-start.3 = (f32[64,128]{1,0:T(8,128)S(1)}, f32[64,128]{1,0:T(8,128)}, u32[]{:S(2)}) copy-start(f32[64,128]{1,0:T(8,128)} %param.13) | copy-start | bytes 98308
  95.4 45.2 %all-to-all-start.1 = ((bf16[16,64,256]{2,1,0:T(8,128)(2,1)}), bf16[16,64,256]{2,1,0:T(8,128)(2,1)S(1)}, u32[]{:S(2)}, u32[]{:S(2)}) async-start(bf16[16,64,256]{2,1,0:T(8,128)(2,1)} %bitcast.25), calls=%async_computation.1 | async-start | bytes 1048576 | tf_op jit(solution)/shard_map/all_to_all | solution.py:88
  142.0 17.1 %all-to-all-start.2 = ((bf16[16,4,64,128]{3,2,1,0:T(8,128)(2,1)}), bf16[16,4,64,128]{3,2,1,0:T(8,128)(2,1)S(1)}, u32[]{:S(2)}, u32[]{:S(2)}) async-start(bf16[16,4,64,128]{3,2,1,0:T(8,128)(2,1)} %broadcast_in_dim.25), calls=%async_computation.2 | async-start | bytes 2097152 | tf_op jit(solution)/shard_map/all_to_all | solution.py:100

commit v2 on v1

v2 whole, which is shorter than its diff:
```python
import math

import jax
import jax.numpy as jnp
from jax import lax
from jax.experimental import pallas as pl
from jax.experimental.pallas import tpu as pltpu
from jax.sharding import Mesh, PartitionSpec as P

HD = 128
TILE = 256

AXES = ("zh", "zl", "yl", "x", "ya", "yb", "c")
SIZES = (4, 2, 2, 4, 2, 2, 2)
NEAR = ("zl", "yl", "x")

momentum_decay = 0.965
curvature_decay = 0.99
clip_scale = 0.04
learn_rate = 0.0006
weight_decay = 0.1


def swap(v, axes, size, flip):
    return lax.ppermute(v, axes, [(i, i ^ flip) for i in range(size)])


def exchange(v, axes):
    return lax.all_to_all(v, axes, 0, 0, tiled=True)


def copies(v, count):
    return jnp.broadcast_to(v[None], (count,) + v.shape)


def attention_kernel(query_ref, key_ref, true_ref, sample_ref, grads_ref):
    tok_count, heads = query_ref.shape[0], query_ref.shape[1] // HD
    to_power = HD ** (-0.5) * math.log2(math.e)
    tiles = tok_count // TILE
    later = lax.broadcasted_iota(jnp.int32, (TILE, TILE), 0) > lax.broadcasted_iota(
        jnp.int32, (TILE, TILE), 1
    )
    totals = [None] * tiles
    for tile in range(tiles):
        start, end = tile * TILE, (tile + 1) * TILE
        attention, cotangents = [], []
        for head in range(heads):
            lanes = slice(head * HD, (head + 1) * HD)
            scores = lax.dot_general(
                key_ref[:end, :],
                query_ref[start:end, lanes],
                (((1,), (1,)), ((), ())),
                preferred_element_type=jnp.float32,
            )
            diagonal = jnp.where(later, -jnp.inf, scores[start:])
            scores = jnp.concatenate((scores[:start], diagonal), axis=0) if start else diagonal
            highest = jnp.max(scores, axis=0, keepdims=True)
            powers = jnp.exp2((scores - highest) * to_power)
            inverse = 1.0 / jnp.sum(powers, axis=0, keepdims=True)
            attention.append((powers * inverse).astype(jnp.bfloat16))
            cotangents.append(
                jnp.concatenate((true_ref[start:end, lanes], sample_ref[start:end, lanes]), axis=1)
            )
        sums = jnp.dot(
            jnp.concatenate(attention, axis=1),
            jnp.concatenate(cotangents, axis=0),
            preferred_element_type=jnp.float32,
        )
        for i in range(tile + 1):
            rows = sums[i * TILE : (i + 1) * TILE]
            totals[i] = rows if totals[i] is None else totals[i] + rows
    for i in range(tiles):
        grads_ref[i * TILE : (i + 1) * TILE, :] = totals[i].astype(grads_ref.dtype)


def attention_grads(query_rows, key_rows, true_cotangent, sample_cotangent):
    whole = pl.BlockSpec(memory_space=pltpu.VMEM)
    return pl.pallas_call(
        attention_kernel,
        in_specs=[whole] * 4,
        out_specs=whole,
        out_shape=jax.ShapeDtypeStruct((key_rows.shape[0], 2 * HD), jnp.bfloat16),
        compiler_params=pltpu.CompilerParams(vmem_limit_bytes=60 * 1024 * 1024),
        cost_estimate=pl.CostEstimate(flops=0, bytes_accessed=0, transcendentals=0),
    )(query_rows, key_rows, true_cotangent, sample_cotangent)


def shards(
    activations, query_rows, key_rows, true_cotangent, sample_cotangent, master, moment, curvature
):
    zh, core = lax.axis_index("zh"), lax.axis_index("c")
    yl, ya, yb = lax.axis_index("yl"), lax.axis_index("ya"), lax.axis_index("yb")
    rows, width = master.shape
    pair = 2 * width
    across = swap(activations, ("ya", "yb"), 4, 3)
    sibling = swap(activations, "c", 2, 1)
    own = attention_grads(query_rows, key_rows, true_cotangent, sample_cotangent)
    state = jnp.stack((master, moment, curvature))
    own, state = lax.optimization_barrier((own, state))
    other = swap(own, "yb", 2, 1)
    moved = tuple(swap(state, "zh", 4, flip) for flip in (1, 2, 3))
    other, across, moved = lax.optimization_barrier((other, across, moved))
    states = jnp.stack((state,) + moved)
    states = jnp.where(zh & 1 == 0, states, jnp.stack([states[i] for i in (1, 0, 3, 2)]))
    states = jnp.where(zh & 2 == 0, states, jnp.stack([states[i] for i in (2, 3, 0, 1)]))

    def whole(half, sibling):
        return jnp.concatenate(
            (jnp.where(core == 0, half, sibling), jnp.where(core == 0, sibling, half)), axis=1
        )

    blocks = whole(activations, sibling), whole(across, swap(across, "c", 2, 1))
    contract = (((0,), (0,)), ((), ()))
    part = [
        lax.dot_general(block, grads, contract, preferred_element_type=jnp.float32)
        for grads in (own, other)
        for block in blocks
    ]
    part = jnp.stack([p.astype(jnp.bfloat16).reshape(16, rows, pair) for p in part], axis=1)
    part, states = lax.optimization_barrier((part, states))
    part = exchange(part, NEAR)
    part = jnp.sum(part.astype(jnp.float32), axis=0).astype(jnp.bfloat16)
    part_own, part_other = part[:2], part[2:]
    part = jnp.stack(
        (jnp.where(yb == 0, part_own, part_other), jnp.where(yb == 0, part_other, part_own))
    )
    part = jnp.broadcast_to(part[None], (4, 2, 2, rows, pair)).reshape(8, 2, rows, pair)
    part = exchange(part, ("zh", "yb"))
    part = jnp.sum(part.reshape(4, 2, 2, rows, pair).astype(jnp.float32), axis=0)
    summed = jnp.where(
        ya == 0,
        jnp.stack((part[0, 0], part[1, 0], part[1, 1], part[0, 1])),
        jnp.stack((part[1, 1], part[0, 1], part[0, 0], part[1, 0])),
    )
    grad_true = summed[..., :width]
    grad_sample = summed[..., width:]
    moment_next = momentum_decay * states[:, 1] + (1.0 - momentum_decay) * grad_true
    curvature_next = (
        curvature_decay * states[:, 2] + (1.0 - curvature_decay) * grad_sample * grad_sample
    )
    ratio = jnp.clip(moment_next / (clip_scale * curvature_next), -1.0, 1.0)
    master_next = states[:, 0] * (1.0 - learn_rate * weight_decay) - learn_rate * ratio
    weights = master_next.astype(jnp.bfloat16)
    weights = exchange(copies(weights, 16), NEAR)
    weights_next = weights.transpose(1, 0, 2, 3).reshape(64 * rows, width)
    mine = lambda v: lax.dynamic_index_in_dim(v, zh, 0, keepdims=False)
    return (mine(master_next), mine(moment_next), mine(curvature_next), weights_next)


def solution(mesh):
    fine = Mesh(mesh.devices.reshape(SIZES), AXES)
    dp, mp = AXES[:4], AXES[4:]
    placed = (P(dp, mp),) * 8
    return jax.shard_map(
        shards,
        mesh=fine,
        in_specs=placed,
        out_specs=(P(dp, mp), P(dp, mp), P(dp, mp), P(None, mp)),
        check_vma=False,
    )
```

time: 161 us -> 139 us (0.86)
  the two profiles are of different devices: /device:TPU:16 before, /device:TPU:1 now
where the time goes in v2:
time: 139 us; the launch traced here: 138 us
  waiting for transfers between devices  67.2 us (48%)
  starting transfers between devices  55.2 us (40%)
  local copies, waits for them, and re-layouts  5.25 us (4%)
  Pallas kernels  4.83 us (3%)
  other arithmetic  2.51 us (2%)
  matrix products  2.5 us (2%)
    all_to_all x3, waiting for transfers between devices, exchange(): return lax.all_to_all(v, axes, 0, 0, tiled=True)  62 us
    ppermute x7, starting transfers between devices, swap(): return lax.ppermute(v, axes, [(i, i ^ flip) for i in range(size)])  35.2 us
    all_to_all x3, starting transfers between devices, exchange(): return lax.all_to_all(v, axes, 0, 0, tiled=True)  19.9 us
    ppermute x7, waiting for transfers between devices, swap(): return lax.ppermute(v, axes, [(i, i ^ flip) for i in range(size)])  5.19 us
    pallas_call x1, Pallas kernels, attention_grads(): pl.pallas_call(attention_kernel, in_specs=[whole] * 4, out_specs=whole, o...  4.83 us
  transfers between devices with their start and end apart: 10, of which 4 were waited for; matrix products, arithmetic and copies ran while one was open for 2% of the time, Pallas kernels for 3%

profile of v2, /device:TPU:1, one launch (start us, length us, event | category | flops | bytes accessed | tf_op | source)
XLA Modules:
  0.0 138.4 jit_solution(7272856760578163005)
XLA Ops:
  0.7 6.8 %collective-permute-start.2 = (bf16[768,512]{1,0:T(8,128)(2,1)}, bf16[768,512]{1,0:T(8,128)(2,1)S(1)}, u32[]{:S(2)}, u32[]{:S(2)}) collective-permute-start(bf16[768,512]{1,0:T(8,128)(2,1)} %param.8), channel_id=1, source_target_pairs={{0,6},{2,4},{4,2},{6,0},{1,7},{3,5},{5,3},{7,1},{8,14},{10,12},{12... | collective-permute-start | bytes 2359304 | tf_op jit(solution)/shard_map/ppermute | solution.py:25
  7.5 4.8 %shard_map.111 = bf16[768,256]{1,0:T(8,128)(2,1)} custom-call(bf16[768,512]{1,0:T(8,128)(2,1)} %query_ref.1, bf16[768,128]{1,0:T(8,128)(2,1)} %key_ref.1, bf16[768,512]{1,0:T(8,128)(2,1)} %true_ref.1, bf16[768,512]{1,0:T(8,128)(2,1)} %sample_ref.1), custom_call_target="tpu_custom_call" | custom-call | tf_op jit(solution)/shard_map/pallas_call | solution.py:78
  12.4 3.8 %collective-permute-start.1 = (bf16[768,256]{1,0:T(8,128)(2,1)}, bf16[768,256]{1,0:T(8,128)(2,1)S(1)}, u32[]{:S(2)}, u32[]{:S(2)}) collective-permute-start(bf16[768,256]{1,0:T(8,128)(2,1)} %shard_map.111), channel_id=1, source_target_pairs={{0,2},{2,0},{1,3},{3,1},{4,6},{6,4},{5,7},{7,5},{8,10},{10,8},{9,1... | collective-permute-start | bytes 1179656 | tf_op jit(solution)/shard_map/ppermute | solution.py:25
  16.2 3.1 %collective-permute-start = (bf16[768,512]{1,0:T(8,128)(2,1)S(1)}, bf16[768,512]{1,0:T(8,128)(2,1)S(1)}, u32[]{:S(2)}, u32[]{:S(2)}) collective-permute-start(bf16[768,512]{1,0:T(8,128)(2,1)S(1)} %copy-done), channel_id=1, source_target_pairs={{0,1},{1,0},{2,3},{3,2},{4,5},{5,4},{6,7},{7,6},{8,9},{9,8},{10,11... | collective-permute-start | bytes 2359304 | tf_op jit(solution)/shard_map/ppermute | solution.py:25
  19.3 5.8 %collective-permute-start.3 = (f32[3,64,128]{2,1,0:T(8,128)S(1)}, f32[3,64,128]{2,1,0:T(8,128)S(1)}, u32[]{:S(2)}, u32[]{:S(2)}) collective-permute-start(f32[3,64,128]{2,1,0:T(8,128)S(1)} %pad_maximum_fusion.8), channel_id=1, source_target_pairs={{0,128},{128,0},{256,384},{384,256},{1,129},{129,1},{257,385},{385... | collective-permute-start | bytes 294920 | tf_op jit(solution)/shard_map/ppermute | solution.py:25
  25.1 8.8 %collective-permute-start.4 = (f32[3,64,128]{2,1,0:T(8,128)S(1)}, f32[3,64,128]{2,1,0:T(8,128)S(1)}, u32[]{:S(2)}, u32[]{:S(2)}) collective-permute-start(f32[3,64,128]{2,1,0:T(8,128)S(1)} %pad_maximum_fusion.8), channel_id=1, source_target_pairs={{0,256},{128,384},{256,0},{384,128},{1,257},{129,385},{257,1},{385... | collective-permute-start | bytes 294920 | tf_op jit(solution)/shard_map/ppermute | solution.py:25
  34.0 4.5 %collective-permute-start.5 = (f32[3,64,128]{2,1,0:T(8,128)S(1)}, f32[3,64,128]{2,1,0:T(8,128)S(1)}, u32[]{:S(2)}, u32[]{:S(2)}) collective-permute-start(f32[3,64,128]{2,1,0:T(8,128)S(1)} %pad_maximum_fusion.8), channel_id=1, source_target_pairs={{0,384},{128,256},{256,128},{384,0},{1,385},{129,257},{257,129},{3... | collective-permute-start | bytes 294920 | tf_op jit(solution)/shard_map/ppermute | solution.py:25
  38.5 5.2 %collective-permute-done.5 = f32[3,64,128]{2,1,0:T(8,128)S(1)} collective-permute-done((f32[3,64,128]{2,1,0:T(8,128)S(1)}, f32[3,64,128]{2,1,0:T(8,128)S(1)}, u32[]{:S(2)}, u32[]{:S(2)}) %collective-permute-start.5) | collective-permute-done | bytes 98336 | tf_op jit(solution)/shard_map/ppermute | solution.py:25
  43.7 2.4 %collective-permute-start.6 = (bf16[768,512]{1,0:T(8,128)(2,1)S(1)}, bf16[768,512]{1,0:T(8,128)(2,1)S(1)}, u32[]{:S(2)}, u32[]{:S(2)}) collective-permute-start(bf16[768,512]{1,0:T(8,128)(2,1)S(1)} %collective-permute-done.2), channel_id=1, source_target_pairs={{0,1},{1,0},{2,3},{3,2},{4,5},{5,4},{6,7},{7,6},{8,9},{9,8},{10,11... | collective-permute-start | bytes 2359304 | tf_op jit(solution)/shard_map/ppermute | solution.py:25
  46.1 0.1 maximum_select_fusion.1
  46.2 0.1 broadcast_select_fusion.3
  46.3 0.8 copy-done.1
  47.1 0.6 convolution_convert_fusion.3
  47.8 0.6 convolution_convert_fusion.1
  48.4 0.1 broadcast_select_fusion.1
  48.5 0.6 convolution_convert_fusion
  49.2 0.6 convolution_convert_fusion.2
  49.8 1.6 %pad_maximum_fusion = bf16[16,4,64,256]{3,2,1,0:T(8,128)(2,1)} fusion(bf16[16,1,64,256]{3,2,1,0:T(8,128)(2,1)S(1)} %bitcast.68, bf16[16,1,64,256]{3,2,1,0:T(8,128)(2,1)S(1)} %bitcast.67, bf16[16,1,64,256]{3,2,1,0:T(8,128)(2,1)S(1)} %bitcast.69, bf16[16,1,64,256]{3,2,1,0:T(8,128)(2,1)S(1)} %bitcast.66), kind=kLoop, calls=%fused_computation | loop fusion | flops 3145728 | bytes 4194304 | tf_op jit(solution)/shard_map/stack | solution.py:119
  51.4 8.5 %all-to-all-start = ((bf16[16,4,64,256]{3,2,1,0:T(8,128)(2,1)}), bf16[16,4,64,256]{3,2,1,0:T(8,128)(2,1)S(1)}, u32[]{:S(2)}, u32[]{:S(2)}) async-start(bf16[16,4,64,256]{3,2,1,0:T(8,128)(2,1)} %pad_maximum_fusion), calls=%async_computation | async-start | bytes 4194304 | tf_op jit(solution)/shard_map/all_to_all | solution.py:29
  59.9 29.8 %all-to-all-done = bf16[16,4,64,256]{3,2,1,0:T(8,128)(2,1)S(1)} async-done(((bf16[16,4,64,256]{3,2,1,0:T(8,128)(2,1)}), bf16[16,4,64,256]{3,2,1,0:T(8,128)(2,1)S(1)}, u32[]{:S(2)}, u32[]{:S(2)}) %all-to-all-start) | async-done | bytes 2097184 | tf_op jit(solution)/shard_map/all_to_all | solution.py:29
  89.7 0.4 reduce_sum.21
  90.1 0.8 broadcast_in_dim.4
  91.0 7.2 %all-to-all-start.1 = ((bf16[8,2,64,256]{3,2,1,0:T(8,128)(2,1)}), bf16[8,2,64,256]{3,2,1,0:T(8,128)(2,1)S(1)}, u32[]{:S(2)}, u32[]{:S(2)}) async-start(bf16[8,2,64,256]{3,2,1,0:T(8,128)(2,1)} %bitcast.23), calls=%async_computation.1 | async-start | bytes 1048576 | tf_op jit(solution)/shard_map/all_to_all | solution.py:29
  98.2 17.9 %all-to-all-done.1 = bf16[8,2,64,256]{3,2,1,0:T(8,128)(2,1)S(1)} async-done(((bf16[8,2,64,256]{3,2,1,0:T(8,128)(2,1)}), bf16[8,2,64,256]{3,2,1,0:T(8,128)(2,1)S(1)}, u32[]{:S(2)}, u32[]{:S(2)}) %all-to-all-start.1) | async-done | bytes 524320 | tf_op jit(solution)/shard_map/all_to_all | solution.py:29
  116.1 0.1 convert_reduce_fusion
  116.2 0.1 fusion.6
  116.3 1.2 broadcast_in_dim.5
  117.5 4.2 %all-to-all-start.2 = ((bf16[16,4,64,128]{3,2,1,0:T(8,128)(2,1)}), bf16[16,4,64,128]{3,2,1,0:T(8,128)(2,1)S(1)}, u32[]{:S(2)}, u32[]{:S(2)}) async-start(bf16[16,4,64,128]{3,2,1,0:T(8,128)(2,1)} %broadcast_in_dim.5), calls=%async_computation.2 | async-start | bytes 2097152 | tf_op jit(solution)/shard_map/all_to_all | solution.py:29
  121.8 0.6 dynamic-slice_bitcast_fusion.2
  122.4 0.6 dynamic-slice_bitcast_fusion
  123.0 14.3 %all-to-all-done.2 = bf16[16,4,64,128]{3,2,1,0:T(8,128)(2,1)S(1)} async-done(((bf16[16,4,64,128]{3,2,1,0:T(8,128)(2,1)}), bf16[16,4,64,128]{3,2,1,0:T(8,128)(2,1)S(1)}, u32[]{:S(2)}, u32[]{:S(2)}) %all-to-all-start.2) | async-done | bytes 1048608 | tf_op jit(solution)/shard_map/all_to_all | solution.py:29
  137.3 1.1 copy.35
  (22 shorter events, 0.2 us)
Async XLA Ops:
  0.6 15.5 %copy-start = (bf16[768,512]{1,0:T(8,128)(2,1)S(1)}, bf16[768,512]{1,0:T(8,128)(2,1)}, u32[]{:S(2)}) copy-start(bf16[768,512]{1,0:T(8,128)(2,1)} %param.8) | copy-start | bytes 2359300
  0.6 11.7 %copy-start.4 = (f32[64,128]{1,0:T(8,128)S(1)}, f32[64,128]{1,0:T(8,128)}, u32[]{:S(2)}) copy-start(f32[64,128]{1,0:T(8,128)} %param.13) | copy-start | bytes 98308
  0.7 11.7 %copy-start.3 = (f32[64,128]{1,0:T(8,128)S(1)}, f32[64,128]{1,0:T(8,128)}, u32[]{:S(2)}) copy-start(f32[64,128]{1,0:T(8,128)} %param.14) | copy-start | bytes 98308
  0.7 11.7 %copy-start.2 = (f32[64,128]{1,0:T(8,128)S(1)}, f32[64,128]{1,0:T(8,128)}, u32[]{:S(2)}) copy-start(f32[64,128]{1,0:T(8,128)} %param.15) | copy-start | bytes 98308
  0.7 43.0 %collective-permute-start.2 = (bf16[768,512]{1,0:T(8,128)(2,1)}, bf16[768,512]{1,0:T(8,128)(2,1)S(1)}, u32[]{:S(2)}, u32[]{:S(2)}) collective-permute-start(bf16[768,512]{1,0:T(8,128)(2,1)} %param.8), channel_id=1, source_target_pairs={{0,6},{2,4},{4,2},{6,0},{1,7},{3,5},{5,3},{7,1},{8,14},{10,12},{12... | collective-permute-start | bytes 2359304 | tf_op jit(solution)/shard_map/ppermute | solution.py:25
  12.4 31.3 %collective-permute-start.1 = (bf16[768,256]{1,0:T(8,128)(2,1)}, bf16[768,256]{1,0:T(8,128)(2,1)S(1)}, u32[]{:S(2)}, u32[]{:S(2)}) collective-permute-start(bf16[768,256]{1,0:T(8,128)(2,1)} %shard_map.111), channel_id=1, source_target_pairs={{0,2},{2,0},{1,3},{3,1},{4,6},{6,4},{5,7},{7,5},{8,10},{10,8},{9,1... | collective-permute-start | bytes 1179656 | tf_op jit(solution)/shard_map/ppermute | solution.py:25
  16.2 30.1 %collective-permute-start = (bf16[768,512]{1,0:T(8,128)(2,1)S(1)}, bf16[768,512]{1,0:T(8,128)(2,1)S(1)}, u32[]{:S(2)}, u32[]{:S(2)}) collective-permute-start(bf16[768,512]{1,0:T(8,128)(2,1)S(1)} %copy-done), channel_id=1, source_target_pairs={{0,1},{1,0},{2,3},{3,2},{4,5},{5,4},{6,7},{7,6},{8,9},{9,8},{10,11... | collective-permute-start | bytes 2359304 | tf_op jit(solution)/shard_map/ppermute | solution.py:25
  19.3 14.7 %collective-permute-start.3 = (f32[3,64,128]{2,1,0:T(8,128)S(1)}, f32[3,64,128]{2,1,0:T(8,128)S(1)}, u32[]{:S(2)}, u32[]{:S(2)}) collective-permute-start(f32[3,64,128]{2,1,0:T(8,128)S(1)} %pad_maximum_fusion.8), channel_id=1, source_target_pairs={{0,128},{128,0},{256,384},{384,256},{1,129},{129,1},{257,385},{385... | collective-permute-start | bytes 294920 | tf_op jit(solution)/shard_map/ppermute | solution.py:25
  25.1 13.3 %collective-permute-start.4 = (f32[3,64,128]{2,1,0:T(8,128)S(1)}, f32[3,64,128]{2,1,0:T(8,128)S(1)}, u32[]{:S(2)}, u32[]{:S(2)}) collective-permute-start(f32[3,64,128]{2,1,0:T(8,128)S(1)} %pad_maximum_fusion.8), channel_id=1, source_target_pairs={{0,256},{128,384},{256,0},{384,128},{1,257},{129,385},{257,1},{385... | collective-permute-start | bytes 294920 | tf_op jit(solution)/shard_map/ppermute | solution.py:25
  34.0 9.7 %collective-permute-start.5 = (f32[3,64,128]{2,1,0:T(8,128)S(1)}, f32[3,64,128]{2,1,0:T(8,128)S(1)}, u32[]{:S(2)}, u32[]{:S(2)}) collective-permute-start(f32[3,64,128]{2,1,0:T(8,128)S(1)} %pad_maximum_fusion.8), channel_id=1, source_target_pairs={{0,384},{128,256},{256,128},{384,0},{1,385},{129,257},{257,129},{3... | collective-permute-start | bytes 294920 | tf_op jit(solution)/shard_map/ppermute | solution.py:25
  43.7 4.7 %collective-permute-start.6 = (bf16[768,512]{1,0:T(8,128)(2,1)S(1)}, bf16[768,512]{1,0:T(8,128)(2,1)S(1)}, u32[]{:S(2)}, u32[]{:S(2)}) collective-permute-start(bf16[768,512]{1,0:T(8,128)(2,1)S(1)} %collective-permute-done.2), channel_id=1, source_target_pairs={{0,1},{1,0},{2,3},{3,2},{4,5},{5,4},{6,7},{7,6},{8,9},{9,8},{10,11... | collective-permute-start | bytes 2359304 | tf_op jit(solution)/shard_map/ppermute | solution.py:25
  46.1 1.0 copy-start.1
  51.4 38.3 %all-to-all-start = ((bf16[16,4,64,256]{3,2,1,0:T(8,128)(2,1)}), bf16[16,4,64,256]{3,2,1,0:T(8,128)(2,1)S(1)}, u32[]{:S(2)}, u32[]{:S(2)}) async-start(bf16[16,4,64,256]{3,2,1,0:T(8,128)(2,1)} %pad_maximum_fusion), calls=%async_computation | async-start | bytes 4194304 | tf_op jit(solution)/shard_map/all_to_all | solution.py:29
  91.0 25.1 %all-to-all-start.1 = ((bf16[8,2,64,256]{3,2,1,0:T(8,128)(2,1)}), bf16[8,2,64,256]{3,2,1,0:T(8,128)(2,1)S(1)}, u32[]{:S(2)}, u32[]{:S(2)}) async-start(bf16[8,2,64,256]{3,2,1,0:T(8,128)(2,1)} %bitcast.23), calls=%async_computation.1 | async-start | bytes 1048576 | tf_op jit(solution)/shard_map/all_to_all | solution.py:29
  117.5 19.8 %all-to-all-start.2 = ((bf16[16,4,64,128]{3,2,1,0:T(8,128)(2,1)}), bf16[16,4,64,128]{3,2,1,0:T(8,128)(2,1)S(1)}, u32[]{:S(2)}, u32[]{:S(2)}) async-start(bf16[16,4,64,128]{3,2,1,0:T(8,128)(2,1)} %broadcast_in_dim.5), calls=%async_computation.2 | async-start | bytes 2097152 | tf_op jit(solution)/shard_map/all_to_all | solution.py:29

commit v3 on v2

--- a/solution.py
+++ b/solution.py
@@ -85,6 +85,49 @@
     )(query_rows, key_rows, true_cotangent, sample_cotangent)
 
 
+def update_kernel(place_ref, part_ref, states_ref, master_ref, moment_ref, curvature_ref, weights_ref):
+    zh, ya = place_ref[0], place_ref[1]
+    width = master_ref.shape[1]
+    for yb in range(2):
+        for side in range(2):
+            block = (2 * ya + yb) ^ (3 * side)
+            summed = part_ref[0, yb, side].astype(jnp.float32)
+            for group in range(1, 4):
+                summed += part_ref[group, yb, side].astype(jnp.float32)
+            grad_true = summed[:, :width]
+            grad_sample = summed[:, width:]
+            state = states_ref[block ^ zh]
+            moment_next = momentum_decay * state[1] + (1.0 - momentum_decay) * grad_true
+            curvature_next = (
+                curvature_decay * state[2] + (1.0 - curvature_decay) * grad_sample * grad_sample
+            )
+            ratio = jnp.clip(moment_next / (clip_scale * curvature_next), -1.0, 1.0)
+            master_next = state[0] * (1.0 - learn_rate * weight_decay) - learn_rate * ratio
+            weights = master_next.astype(jnp.bfloat16)
+            for copy in range(weights_ref.shape[0]):
+                weights_ref[copy, block] = weights
+
+            @pl.when(block == zh)
+            def _():
+                master_ref[...] = master_next
+                moment_ref[...] = moment_next
+                curvature_ref[...] = curvature_next
+
+
+def update(place, part, states):
+    rows, width = states.shape[2:]
+    whole = pl.BlockSpec(memory_space=pltpu.VMEM)
+    mine = jax.ShapeDtypeStruct((rows, width), jnp.float32)
+    return pl.pallas_call(
+        update_kernel,
+        in_specs=[pl.BlockSpec(memory_space=pltpu.SMEM), whole, whole],
+        out_specs=[whole] * 4,
+        out_shape=[mine, mine, mine, jax.ShapeDtypeStruct((16, 4, rows, width), jnp.bfloat16)],
+        compiler_params=pltpu.CompilerParams(vmem_limit_bytes=16 * 1024 * 1024),
+        cost_estimate=pl.CostEstimate(flops=2**21, bytes_accessed=2**21, transcendentals=0),
+    )(place, part, states)
+
+
 def shards(
     activations, query_rows, key_rows, true_cotangent, sample_cotangent, master, moment, curvature
 ):
@@ -101,8 +144,6 @@
     moved = tuple(swap(state, "zh", 4, flip) for flip in (1, 2, 3))
     other, across, moved = lax.optimization_barrier((other, across, moved))
     states = jnp.stack((state,) + moved)
-    states = jnp.where(zh & 1 == 0, states, jnp.stack([states[i] for i in (1, 0, 3, 2)]))
-    states = jnp.where(zh & 2 == 0, states, jnp.stack([states[i] for i in (2, 3, 0, 1)]))
 
     def whole(half, sibling):
         return jnp.concatenate(
@@ -117,34 +158,21 @@
         for block in blocks
     ]
     part = jnp.stack([p.astype(jnp.bfloat16).reshape(16, rows, pair) for p in part], axis=1)
-    part, states = lax.optimization_barrier((part, states))
+    part, states, place, even = lax.optimization_barrier(
+        (part, states, jnp.stack((zh, ya)).astype(jnp.int32), yb == 0)
+    )
     part = exchange(part, NEAR)
     part = jnp.sum(part.astype(jnp.float32), axis=0).astype(jnp.bfloat16)
     part_own, part_other = part[:2], part[2:]
     part = jnp.stack(
-        (jnp.where(yb == 0, part_own, part_other), jnp.where(yb == 0, part_other, part_own))
+        (jnp.where(even, part_own, part_other), jnp.where(even, part_other, part_own))
     )
     part = jnp.broadcast_to(part[None], (4, 2, 2, rows, pair)).reshape(8, 2, rows, pair)
     part = exchange(part, ("zh", "yb"))
-    part = jnp.sum(part.reshape(4, 2, 2, rows, pair).astype(jnp.float32), axis=0)
-    summed = jnp.where(
-        ya == 0,
-        jnp.stack((part[0, 0], part[1, 0], part[1, 1], part[0, 1])),
-        jnp.stack((part[1, 1], part[0, 1], part[0, 0], part[1, 0])),
-    )
-    grad_true = summed[..., :width]
-    grad_sample = summed[..., width:]
-    moment_next = momentum_decay * states[:, 1] + (1.0 - momentum_decay) * grad_true
-    curvature_next = (
-        curvature_decay * states[:, 2] + (1.0 - curvature_decay) * grad_sample * grad_sample
-    )
-    ratio = jnp.clip(moment_next / (clip_scale * curvature_next), -1.0, 1.0)
-    master_next = states[:, 0] * (1.0 - learn_rate * weight_decay) - learn_rate * ratio
-    weights = master_next.astype(jnp.bfloat16)
-    weights = exchange(copies(weights, 16), NEAR)
+    *ours, weights = update(place, part.reshape(4, 2, 2, rows, pair), states)
+    weights = exchange(weights, NEAR)
     weights_next = weights.transpose(1, 0, 2, 3).reshape(64 * rows, width)
-    mine = lambda v: lax.dynamic_index_in_dim(v, zh, 0, keepdims=False)
-    return (mine(master_next), mine(moment_next), mine(curvature_next), weights_next)
+    return (*ours, weights_next)
 
 
 def solution(mesh):

time: 139 us -> 135 us (0.971)
  blocking collectives: 0 us -> 81.5 us
  waiting for transfers between devices: 67.2 us -> 6.63 us
  starting transfers between devices: 55.2 us -> 34.7 us
  local copies, waits for them, and re-layouts: 5.25 us -> 1.49 us
  other arithmetic: 2.51 us -> 1.01 us
    all_to_all x0 -> x3, blocking collectives: none -> 81.5 us  [exchange(): return lax.all_to_all(v, axes, 0, 0, tiled=True)]
    all_to_all x3 -> x0, waiting for transfers between devices: 62 us -> none  [exchange(): return lax.all_to_all(v, axes, 0, 0, tiled=True)]
    all_to_all x3 -> x0, starting transfers between devices: 19.9 us -> none  [exchange(): return lax.all_to_all(v, axes, 0, 0, tiled=True)]
    ppermute x7, waiting for transfers between devices: 5.19 us -> 6.63 us  [swap(): return lax.ppermute(v, axes, [(i, i ^ flip) for i in range(size)])]
    pallas_call x0 -> x1, Pallas kernels: none -> 1.39 us  [update(): pl.pallas_call(update_kernel, in_specs=[pl.BlockSpec(memory_space=pltpu.S...]
  transfers between devices with their start and end apart: 10 -> 7, of which waited for: 4 -> 3; matrix products, arithmetic and copies ran while one was open for 2% -> 1% of each run, Pallas kernels for 3% -> 4%
where the time goes in v3:
time: 135 us
  blocking collectives  81.5 us (60%)
  starting transfers between devices  34.7 us (26%)
  waiting for transfers between devices  6.63 us (5%)
  Pallas kernels  6.22 us (5%)
  matrix products  2.5 us (2%)
  local copies, waits for them, and re-layouts  1.49 us (1%)
    all_to_all x3, blocking collectives, exchange(): return lax.all_to_all(v, axes, 0, 0, tiled=True)  81.5 us
    ppermute x7, starting transfers between devices, swap(): return lax.ppermute(v, axes, [(i, i ^ flip) for i in range(size)])  34.7 us
    ppermute x7, waiting for transfers between devices, swap(): return lax.ppermute(v, axes, [(i, i ^ flip) for i in range(size)])  6.63 us
    pallas_call x1, Pallas kernels, attention_grads(): pl.pallas_call(attention_kernel, in_specs=[whole] * 4, out_specs=whole, o...  4.83 us
  transfers between devices with their start and end apart: 7, of which 3 were waited for; matrix products, arithmetic and copies ran while one was open for 1% of the time, Pallas kernels for 4%

profile of v3, /device:TPU:1, one launch (start us, length us, event | category | flops | bytes accessed | tf_op | source)
XLA Modules:
  0.0 134.9 jit_solution(1398454931308105266)
XLA Ops:
  0.6 0.0 copy-start
  0.7 6.8 %collective-permute-start.2 = (bf16[768,512]{1,0:T(8,128)(2,1)}, bf16[768,512]{1,0:T(8,128)(2,1)S(1)}, u32[]{:S(2)}, u32[]{:S(2)}) collective-permute-start(bf16[768,512]{1,0:T(8,128)(2,1)} %param.8), channel_id=1, source_target_pairs={{0,6},{2,4},{4,2},{6,0},{1,7},{3,5},{5,3},{7,1},{8,14},{10,12},{12... | collective-permute-start | bytes 2359304 | tf_op jit(solution)/shard_map/ppermute | solution.py:25
  7.5 4.0 %collective-permute-start = (bf16[768,512]{1,0:T(8,128)(2,1)}, bf16[768,512]{1,0:T(8,128)(2,1)S(1)}, u32[]{:S(2)}, u32[]{:S(2)}) collective-permute-start(bf16[768,512]{1,0:T(8,128)(2,1)} %param.8), channel_id=1, source_target_pairs={{0,1},{1,0},{2,3},{3,2},{4,5},{5,4},{6,7},{7,6},{8,9},{9,8},{10,11... | collective-permute-start | bytes 2359304 | tf_op jit(solution)/shard_map/ppermute | solution.py:25
  11.5 4.8 %shard_map.111 = bf16[768,256]{1,0:T(8,128)(2,1)} custom-call(bf16[768,512]{1,0:T(8,128)(2,1)} %query_ref.1, bf16[768,128]{1,0:T(8,128)(2,1)} %key_ref.1, bf16[768,512]{1,0:T(8,128)(2,1)} %true_ref.1, bf16[768,512]{1,0:T(8,128)(2,1)} %sample_ref.1), custom_call_target="tpu_custom_call" | custom-call | tf_op jit(solution)/shard_map/pallas_call | solution.py:78
  16.4 0.0 copy-done.2
  16.4 2.8 %collective-permute-start.1 = (bf16[768,256]{1,0:T(8,128)(2,1)}, bf16[768,256]{1,0:T(8,128)(2,1)S(1)}, u32[]{:S(2)}, u32[]{:S(2)}) collective-permute-start(bf16[768,256]{1,0:T(8,128)(2,1)} %shard_map.111), channel_id=1, source_target_pairs={{0,2},{2,0},{1,3},{3,1},{4,6},{6,4},{5,7},{7,5},{8,10},{10,8},{9,1... | collective-permute-start | bytes 1179656 | tf_op jit(solution)/shard_map/ppermute | solution.py:25
  19.2 5.8 %collective-permute-start.3 = (f32[3,64,128]{2,1,0:T(8,128)S(1)}, f32[3,64,128]{2,1,0:T(8,128)S(1)}, u32[]{:S(2)}, u32[]{:S(2)}) collective-permute-start(f32[3,64,128]{2,1,0:T(8,128)S(1)} %pad_maximum_fusion.9), channel_id=1, source_target_pairs={{0,128},{128,0},{256,384},{384,256},{1,129},{129,1},{257,385},{385... | collective-permute-start | bytes 294920 | tf_op jit(solution)/shard_map/ppermute | solution.py:25
  25.0 8.8 %collective-permute-start.4 = (f32[3,64,128]{2,1,0:T(8,128)S(1)}, f32[3,64,128]{2,1,0:T(8,128)S(1)}, u32[]{:S(2)}, u32[]{:S(2)}) collective-permute-start(f32[3,64,128]{2,1,0:T(8,128)S(1)} %pad_maximum_fusion.9), channel_id=1, source_target_pairs={{0,256},{128,384},{256,0},{384,128},{1,257},{129,385},{257,1},{385... | collective-permute-start | bytes 294920 | tf_op jit(solution)/shard_map/ppermute | solution.py:25
  33.8 0.0 collective-permute-done.3
  33.8 4.1 %collective-permute-start.5 = (f32[3,64,128]{2,1,0:T(8,128)S(1)}, f32[3,64,128]{2,1,0:T(8,128)S(1)}, u32[]{:S(2)}, u32[]{:S(2)}) collective-permute-start(f32[3,64,128]{2,1,0:T(8,128)S(1)} %pad_maximum_fusion.9), channel_id=1, source_target_pairs={{0,384},{128,256},{256,128},{384,0},{1,385},{129,257},{257,129},{3... | collective-permute-start | bytes 294920 | tf_op jit(solution)/shard_map/ppermute | solution.py:25
  38.0 0.1 pad_add_fusion.place_ref
  38.1 0.0 collective-permute-done.4
  38.1 5.2 %collective-permute-done.5 = f32[3,64,128]{2,1,0:T(8,128)S(1)} collective-permute-done((f32[3,64,128]{2,1,0:T(8,128)S(1)}, f32[3,64,128]{2,1,0:T(8,128)S(1)}, u32[]{:S(2)}, u32[]{:S(2)}) %collective-permute-start.5) | collective-permute-done | bytes 98336 | tf_op jit(solution)/shard_map/ppermute | solution.py:25
  43.2 1.4 %collective-permute-done.1 = bf16[768,256]{1,0:T(8,128)(2,1)S(1)} collective-permute-done((bf16[768,256]{1,0:T(8,128)(2,1)}, bf16[768,256]{1,0:T(8,128)(2,1)S(1)}, u32[]{:S(2)}, u32[]{:S(2)}) %collective-permute-start.1) | collective-permute-done | bytes 393248 | tf_op jit(solution)/shard_map/ppermute | solution.py:25
  44.6 0.0 collective-permute-done.2
  44.6 2.3 %collective-permute-start.6 = (bf16[768,512]{1,0:T(8,128)(2,1)S(1)}, bf16[768,512]{1,0:T(8,128)(2,1)S(1)}, u32[]{:S(2)}, u32[]{:S(2)}) collective-permute-start(bf16[768,512]{1,0:T(8,128)(2,1)S(1)} %collective-permute-done.2), channel_id=1, source_target_pairs={{0,1},{1,0},{2,3},{3,2},{4,5},{5,4},{6,7},{7,6},{8,9},{9,8},{10,11... | collective-permute-start | bytes 2359304 | tf_op jit(solution)/shard_map/ppermute | solution.py:25
  47.0 0.0 collective-permute-done
  47.0 0.1 broadcast_select_fusion.3
  47.2 0.6 convolution_convert_fusion.3
  47.8 0.4 copy-done.6
  48.2 0.6 convolution_convert_fusion.1
  48.8 0.1 collective-permute-done.6
  48.9 0.1 broadcast_select_fusion.1
  49.0 0.6 convolution_convert_fusion
  49.6 0.6 convolution_convert_fusion.2
  50.2 0.3 pad_maximum_fusion
  50.5 34.8 %all_to_all.15 = bf16[16,4,64,256]{3,2,1,0:T(8,128)(2,1)S(1)} all-to-all(bf16[16,4,64,256]{3,2,1,0:T(8,128)(2,1)S(1)} %pad_maximum_fusion), channel_id=1, replica_groups=mesh['zh'=4,'zl'=2,'yl'=2,'x'=4,'ya'=2,'yb'=2,'c'=2] {'zl','yl','x'}, dimensions={0} | all-to-all | bytes 4194304 | tf_op jit(solution)/shard_map/all_to_all | solution.py:29
  85.3 0.4 reduce_sum.12
  85.8 28.2 %all_to_all.16 = bf16[8,2,64,256]{3,2,1,0:T(8,128)(2,1)S(1)} all-to-all(bf16[8,2,64,256]{3,2,1,0:T(8,128)(2,1)S(1)} %bitcast.35), channel_id=1, replica_groups=mesh['zh'=4,'zl'=2,'yl'=2,'x'=4,'ya'=2,'yb'=2,'c'=2] {'zh','yb'}, dimensions={0} | all-to-all | bytes 1048576 | tf_op jit(solution)/shard_map/all_to_all | solution.py:29
  114.0 1.4 %shard_map.112 = (f32[64,128]{1,0:T(8,128)}, f32[64,128]{1,0:T(8,128)}, f32[64,128]{1,0:T(8,128)}, bf16[16,4,64,128]{3,2,1,0:T(8,128)(2,1)S(1)}) custom-call(s32[2]{0:T(128)S(1)} %pad_add_fusion.place_ref, bf16[4,2,2,64,256]{4,3,2,1,0:T(8,128)(2,1)S(1)} %bitcast.33, f32[4,3,64,128]{3,2,1,0:T(8,128)S(1)} %pad_maximum_fusion.7.states_ref), custom_call_target="tpu_custom_call" | custom-call | flops 2097152 | bytes 2097152 | tf_op jit(solution)/shard_map/pallas_call | solution.py:121
  115.4 18.5 %all_to_all.17 = bf16[16,4,64,128]{3,2,1,0:T(8,128)(2,1)S(1)} all-to-all(bf16[16,4,64,128]{3,2,1,0:T(8,128)(2,1)S(1)} %get-tuple-element.33), channel_id=1, replica_groups=mesh['zh'=4,'zl'=2,'yl'=2,'x'=4,'ya'=2,'yb'=2,'c'=2] {'zl','yl','x'}, dimensions={0} | all-to-all | bytes 2097152 | tf_op jit(solution)/shard_map/all_to_all | solution.py:29
  133.9 1.1 copy.17
  (16 shorter events, 0.1 us)
Async XLA Ops:
  0.6 46.4 %copy-start = (bf16[768,512]{1,0:T(8,128)(2,1)S(1)}, bf16[768,512]{1,0:T(8,128)(2,1)}, u32[]{:S(2)}) copy-start(bf16[768,512]{1,0:T(8,128)(2,1)} %param.8) | copy-start | bytes 2359300
  0.6 15.7 %copy-start.4 = (f32[64,128]{1,0:T(8,128)S(1)}, f32[64,128]{1,0:T(8,128)}, u32[]{:S(2)}) copy-start(f32[64,128]{1,0:T(8,128)} %param.13) | copy-start | bytes 98308
  0.7 15.7 %copy-start.3 = (f32[64,128]{1,0:T(8,128)S(1)}, f32[64,128]{1,0:T(8,128)}, u32[]{:S(2)}) copy-start(f32[64,128]{1,0:T(8,128)} %param.14) | copy-start | bytes 98308
  0.7 15.7 %copy-start.2 = (f32[64,128]{1,0:T(8,128)S(1)}, f32[64,128]{1,0:T(8,128)}, u32[]{:S(2)}) copy-start(f32[64,128]{1,0:T(8,128)} %param.15) | copy-start | bytes 98308
  0.7 43.9 %collective-permute-start.2 = (bf16[768,512]{1,0:T(8,128)(2,1)}, bf16[768,512]{1,0:T(8,128)(2,1)S(1)}, u32[]{:S(2)}, u32[]{:S(2)}) collective-permute-start(bf16[768,512]{1,0:T(8,128)(2,1)} %param.8), channel_id=1, source_target_pairs={{0,6},{2,4},{4,2},{6,0},{1,7},{3,5},{5,3},{7,1},{8,14},{10,12},{12... | collective-permute-start | bytes 2359304 | tf_op jit(solution)/shard_map/ppermute | solution.py:25
  7.5 39.5 %collective-permute-start = (bf16[768,512]{1,0:T(8,128)(2,1)}, bf16[768,512]{1,0:T(8,128)(2,1)S(1)}, u32[]{:S(2)}, u32[]{:S(2)}) collective-permute-start(bf16[768,512]{1,0:T(8,128)(2,1)} %param.8), channel_id=1, source_target_pairs={{0,1},{1,0},{2,3},{3,2},{4,5},{5,4},{6,7},{7,6},{8,9},{9,8},{10,11... | collective-permute-start | bytes 2359304 | tf_op jit(solution)/shard_map/ppermute | solution.py:25
  16.4 30.8 %copy-start.1 = (bf16[768,256]{1,0:T(8,128)(2,1)S(1)}, bf16[768,256]{1,0:T(8,128)(2,1)}, u32[]{:S(2)}) copy-start(bf16[768,256]{1,0:T(8,128)(2,1)} %shard_map.111) | copy-start | bytes 1179652
  16.4 28.2 %collective-permute-start.1 = (bf16[768,256]{1,0:T(8,128)(2,1)}, bf16[768,256]{1,0:T(8,128)(2,1)S(1)}, u32[]{:S(2)}, u32[]{:S(2)}) collective-permute-start(bf16[768,256]{1,0:T(8,128)(2,1)} %shard_map.111), channel_id=1, source_target_pairs={{0,2},{2,0},{1,3},{3,1},{4,6},{6,4},{5,7},{7,5},{8,10},{10,8},{9,1... | collective-permute-start | bytes 1179656 | tf_op jit(solution)/shard_map/ppermute | solution.py:25
  19.2 14.7 %collective-permute-start.3 = (f32[3,64,128]{2,1,0:T(8,128)S(1)}, f32[3,64,128]{2,1,0:T(8,128)S(1)}, u32[]{:S(2)}, u32[]{:S(2)}) collective-permute-start(f32[3,64,128]{2,1,0:T(8,128)S(1)} %pad_maximum_fusion.9), channel_id=1, source_target_pairs={{0,128},{128,0},{256,384},{384,256},{1,129},{129,1},{257,385},{385... | collective-permute-start | bytes 294920 | tf_op jit(solution)/shard_map/ppermute | solution.py:25
  25.0 13.1 %collective-permute-start.4 = (f32[3,64,128]{2,1,0:T(8,128)S(1)}, f32[3,64,128]{2,1,0:T(8,128)S(1)}, u32[]{:S(2)}, u32[]{:S(2)}) collective-permute-start(f32[3,64,128]{2,1,0:T(8,128)S(1)} %pad_maximum_fusion.9), channel_id=1, source_target_pairs={{0,256},{128,384},{256,0},{384,128},{1,257},{129,385},{257,1},{385... | collective-permute-start | bytes 294920 | tf_op jit(solution)/shard_map/ppermute | solution.py:25
  33.8 9.4 %collective-permute-start.5 = (f32[3,64,128]{2,1,0:T(8,128)S(1)}, f32[3,64,128]{2,1,0:T(8,128)S(1)}, u32[]{:S(2)}, u32[]{:S(2)}) collective-permute-start(f32[3,64,128]{2,1,0:T(8,128)S(1)} %pad_maximum_fusion.9), channel_id=1, source_target_pairs={{0,384},{128,256},{256,128},{384,0},{1,385},{129,257},{257,129},{3... | collective-permute-start | bytes 294920 | tf_op jit(solution)/shard_map/ppermute | solution.py:25
  44.6 2.4 %copy-start.5 = (bf16[768,256]{1,0:T(8,128)(2,1)}, bf16[768,256]{1,0:T(8,128)(2,1)S(1)}, u32[]{:S(2)}) copy-start(bf16[768,256]{1,0:T(8,128)(2,1)S(1)} %collective-permute-done.1) | copy-start | bytes 1179652
  44.6 4.2 %collective-permute-start.6 = (bf16[768,512]{1,0:T(8,128)(2,1)S(1)}, bf16[768,512]{1,0:T(8,128)(2,1)S(1)}, u32[]{:S(2)}, u32[]{:S(2)}) collective-permute-start(bf16[768,512]{1,0:T(8,128)(2,1)S(1)} %collective-permute-done.2), channel_id=1, source_target_pairs={{0,1},{1,0},{2,3},{3,2},{4,5},{5,4},{6,7},{7,6},{8,9},{9,8},{10,11... | collective-permute-start | bytes 2359304 | tf_op jit(solution)/shard_map/ppermute | solution.py:25
  47.2 1.0 copy-start.6

commit v4 on v3

--- a/solution.py
+++ b/solution.py
@@ -12,7 +12,7 @@
 
 AXES = ("zh", "zl", "yl", "x", "ya", "yb", "c")
 SIZES = (4, 2, 2, 4, 2, 2, 2)
-NEAR = ("zl", "yl", "x")
+NEAR = ("zl", "x", "yl")
 
 momentum_decay = 0.965
 curvature_decay = 0.99
@@ -85,6 +85,62 @@
     )(query_rows, key_rows, true_cotangent, sample_cotangent)
 
 
+def products_kernel(
+    core_ref, own, own_sibling, across, across_sibling, grads, other, part, halves, both, sums, sems
+):
+    rows, pair = sums.shape[3:]
+    loads = [
+        pltpu.make_async_copy(grads, both.at[:, :pair], sems.at[4]),
+        pltpu.make_async_copy(other, both.at[:, pair:], sems.at[5]),
+    ]
+    for i, half in enumerate((own, own_sibling, across, across_sibling)):
+        loads.append(pltpu.make_async_copy(half, halves.at[i], sems.at[i]))
+    for load in loads:
+        load.start()
+    loads[0].wait()
+    loads[1].wait()
+    stores = []
+    for i in range(4):
+        loads[2 + i].wait()
+        summed = lax.dot_general(
+            halves[i], both[...], (((0,), (0,)), ((), ())), preferred_element_type=jnp.float32
+        ).astype(sums.dtype)
+        for block in range(8):
+            yl, x = block // 4, block % 4
+            for head in range(2):
+                sums[i, 2 * x + yl, head] = summed[
+                    block * rows : (block + 1) * rows, head * pair : (head + 1) * pair
+                ]
+        side, zl = i // 2, core_ref[0] ^ (i % 2)
+        stores.append(
+            pltpu.make_async_copy(sums.at[i], part.at[pl.ds(8 * zl, 8), :, side], sems.at[6 + i])
+        )
+        stores[-1].start()
+    for store in stores:
+        store.wait()
+
+
+def products(core, own_block, across_block, own, other):
+    anywhere = pl.BlockSpec(memory_space=pl.ANY)
+    tok_count, half = own_block[0].shape
+    pair = own.shape[1]
+    rows = half // 8
+    return pl.pallas_call(
+        products_kernel,
+        in_specs=[pl.BlockSpec(memory_space=pltpu.SMEM)] + [anywhere] * 6,
+        out_specs=anywhere,
+        out_shape=jax.ShapeDtypeStruct((16, 2, 2, rows, pair), jnp.bfloat16),
+        scratch_shapes=[
+            pltpu.VMEM((4, tok_count, half), jnp.bfloat16),
+            pltpu.VMEM((tok_count, 2 * pair), jnp.bfloat16),
+            pltpu.VMEM((4, 8, 2, rows, pair), jnp.bfloat16),
+            pltpu.SemaphoreType.DMA((10,)),
+        ],
+        compiler_params=pltpu.CompilerParams(vmem_limit_bytes=60 * 1024 * 1024),
+        cost_estimate=pl.CostEstimate(flops=2**31, bytes_accessed=2**22, transcendentals=0),
+    )(core.astype(jnp.int32)[None], *own_block, *across_block, own, other)
+
+
 def update_kernel(place_ref, part_ref, states_ref, master_ref, moment_ref, curvature_ref, weights_ref):
     zh, ya = place_ref[0], place_ref[1]
     width = master_ref.shape[1]
@@ -145,19 +201,8 @@
     other, across, moved = lax.optimization_barrier((other, across, moved))
     states = jnp.stack((state,) + moved)
 
-    def whole(half, sibling):
-        return jnp.concatenate(
-            (jnp.where(core == 0, half, sibling), jnp.where(core == 0, sibling, half)), axis=1
-        )
-
-    blocks = whole(activations, sibling), whole(across, swap(across, "c", 2, 1))
-    contract = (((0,), (0,)), ((), ()))
-    part = [
-        lax.dot_general(block, grads, contract, preferred_element_type=jnp.float32)
-        for grads in (own, other)
-        for block in blocks
-    ]
-    part = jnp.stack([p.astype(jnp.bfloat16).reshape(16, rows, pair) for p in part], axis=1)
+    part = products(core, (activations, sibling), (across, swap(across, "c", 2, 1)), own, other)
+    part = part.reshape(16, 4, rows, pair)
     part, states, place, even = lax.optimization_barrier(
         (part, states, jnp.stack((zh, ya)).astype(jnp.int32), yb == 0)
     )
@@ -171,7 +216,8 @@
     part = exchange(part, ("zh", "yb"))
     *ours, weights = update(place, part.reshape(4, 2, 2, rows, pair), states)
     weights = exchange(weights, NEAR)
-    weights_next = weights.transpose(1, 0, 2, 3).reshape(64 * rows, width)
+    weights_next = weights.reshape(2, 4, 2, 4, rows, width).transpose(3, 0, 2, 1, 4, 5)
+    weights_next = weights_next.reshape(64 * rows, width)
     return (*ours, weights_next)
 
 

time: 135 us -> 134 us (level); the launches traced: 135 us -> 131 us
  Pallas kernels: 6.22 us -> 10.9 us
  blocking collectives: 81.5 us -> 77.2 us
  matrix products: 2.5 us -> 0 us
    pallas_call x0 -> x1, Pallas kernels: none -> 4.65 us  [products(): pl.pallas_call(products_kernel, in_specs=[pl.BlockSpec(memory_space=pltpu...]
    all_to_all x3, blocking collectives: 81.5 us -> 77.2 us  [exchange(): return lax.all_to_all(v, axes, 0, 0, tiled=True)]
    dot_general x4 -> x0, matrix products: 2.5 us -> none  [shards(): lax.dot_general(block, grads, contract, preferred_element_type=jnp.float32)]
  transfers between devices with their start and end apart: 7 -> 7, of which waited for: 3 -> 3; matrix products, arithmetic and copies ran while one was open for 1% -> 0% of each run, Pallas kernels for 4% -> 4%
where the time goes in v4:
time: 134 us; the launch traced here: 131 us
  blocking collectives  77.2 us (58%)
  starting transfers between devices  33.4 us (25%)
  Pallas kernels  10.9 us (8%)
  waiting for transfers between devices  7.21 us (5%)
    all_to_all x3, blocking collectives, exchange(): return lax.all_to_all(v, axes, 0, 0, tiled=True)  77.2 us
    ppermute x7, starting transfers between devices, swap(): return lax.ppermute(v, axes, [(i, i ^ flip) for i in range(size)])  33.4 us
    ppermute x7, waiting for transfers between devices, swap(): return lax.ppermute(v, axes, [(i, i ^ flip) for i in range(size)])  7.21 us
    pallas_call x1, Pallas kernels, attention_grads(): pl.pallas_call(attention_kernel, in_specs=[whole] * 4, out_specs=whole, o...  4.84 us
    pallas_call x1, Pallas kernels, products(): pl.pallas_call(products_kernel, in_specs=[pl.BlockSpec(memory_space=pltpu...  4.65 us
  transfers between devices with their start and end apart: 7, of which 3 were waited for; matrix products, arithmetic and copies ran while one was open for 0% of the time, Pallas kernels for 4%

profile of v4, /device:TPU:1, one launch (start us, length us, event | category | flops | bytes accessed | tf_op | source)
XLA Modules:
  0.0 131.2 jit_solution(9706719588262939141)
XLA Ops:
  0.6 0.0 copy-start.3
  0.6 0.0 copy-start.2
  0.7 0.0 copy-start.1
  0.7 0.0 copy-start
  0.7 6.8 %collective-permute-start.2 = (bf16[768,512]{1,0:T(8,128)(2,1)}, bf16[768,512]{1,0:T(8,128)(2,1)S(1)}, u32[]{:S(2)}, u32[]{:S(2)}) collective-permute-start(bf16[768,512]{1,0:T(8,128)(2,1)} %own.1), channel_id=1, source_target_pairs={{0,6},{2,4},{4,2},{6,0},{1,7},{3,5},{5,3},{7,1},{8,14},{10,12},{12... | collective-permute-start | bytes 2359304 | tf_op jit(solution)/shard_map/ppermute | solution.py:25
  7.5 4.8 %shard_map.111.grads = bf16[768,256]{1,0:T(8,128)(2,1)} custom-call(bf16[768,512]{1,0:T(8,128)(2,1)} %query_ref.1, bf16[768,128]{1,0:T(8,128)(2,1)} %key_ref.1, bf16[768,512]{1,0:T(8,128)(2,1)} %true_ref.1, bf16[768,512]{1,0:T(8,128)(2,1)} %sample_ref.1), custom_call_target="tpu_custom_call" | custom-call | tf_op jit(solution)/shard_map/pallas_call | solution.py:78
  12.4 0.0 copy-done.2
  12.4 0.0 copy-done.1
  12.4 3.8 %collective-permute-start.1 = (bf16[768,256]{1,0:T(8,128)(2,1)}, bf16[768,256]{1,0:T(8,128)(2,1)S(1)}, u32[]{:S(2)}, u32[]{:S(2)}) collective-permute-start(bf16[768,256]{1,0:T(8,128)(2,1)} %shard_map.111.grads), channel_id=1, source_target_pairs={{0,2},{2,0},{1,3},{3,1},{4,6},{6,4},{5,7},{7,5},{8,10},{10,8},{9,1... | collective-permute-start | bytes 1179656 | tf_op jit(solution)/shard_map/ppermute | solution.py:25
  16.2 5.8 %collective-permute-start.3 = (f32[3,64,128]{2,1,0:T(8,128)S(1)}, f32[3,64,128]{2,1,0:T(8,128)S(1)}, u32[]{:S(2)}, u32[]{:S(2)}) collective-permute-start(f32[3,64,128]{2,1,0:T(8,128)S(1)} %pad_maximum_fusion.2), channel_id=1, source_target_pairs={{0,128},{128,0},{256,384},{384,256},{1,129},{129,1},{257,385},{385... | collective-permute-start | bytes 294920 | tf_op jit(solution)/shard_map/ppermute | solution.py:25
  22.0 8.8 %collective-permute-start.4 = (f32[3,64,128]{2,1,0:T(8,128)S(1)}, f32[3,64,128]{2,1,0:T(8,128)S(1)}, u32[]{:S(2)}, u32[]{:S(2)}) collective-permute-start(f32[3,64,128]{2,1,0:T(8,128)S(1)} %pad_maximum_fusion.2), channel_id=1, source_target_pairs={{0,256},{128,384},{256,0},{384,128},{1,257},{129,385},{257,1},{385... | collective-permute-start | bytes 294920 | tf_op jit(solution)/shard_map/ppermute | solution.py:25
  30.8 1.9 %collective-permute-start.5 = (f32[3,64,128]{2,1,0:T(8,128)S(1)}, f32[3,64,128]{2,1,0:T(8,128)S(1)}, u32[]{:S(2)}, u32[]{:S(2)}) collective-permute-start(f32[3,64,128]{2,1,0:T(8,128)S(1)} %pad_maximum_fusion.2), channel_id=1, source_target_pairs={{0,384},{128,256},{256,128},{384,0},{1,385},{129,257},{257,129},{3... | collective-permute-start | bytes 294920 | tf_op jit(solution)/shard_map/ppermute | solution.py:25
  32.8 0.0 collective-permute-done.3
  32.8 3.7 %collective-permute-start = (bf16[768,512]{1,0:T(8,128)(2,1)S(1)}, bf16[768,512]{1,0:T(8,128)(2,1)S(1)}, u32[]{:S(2)}, u32[]{:S(2)}) collective-permute-start(bf16[768,512]{1,0:T(8,128)(2,1)S(1)} %copy-done.3), channel_id=1, source_target_pairs={{0,1},{1,0},{2,3},{3,2},{4,5},{5,4},{6,7},{7,6},{8,9},{9,8},{10,11... | collective-permute-start | bytes 2359304 | tf_op jit(solution)/shard_map/ppermute | solution.py:25
  36.5 0.0 collective-permute-done.4
  36.5 4.0 %collective-permute-done.5 = f32[3,64,128]{2,1,0:T(8,128)S(1)} collective-permute-done((f32[3,64,128]{2,1,0:T(8,128)S(1)}, f32[3,64,128]{2,1,0:T(8,128)S(1)}, u32[]{:S(2)}, u32[]{:S(2)}) %collective-permute-start.5) | collective-permute-done | bytes 98336 | tf_op jit(solution)/shard_map/ppermute | solution.py:25
  40.5 0.0 collective-permute-done.1.other
  40.5 1.3 collective-permute-done.2.across
  41.8 2.5 %collective-permute-start.6 = (bf16[768,512]{1,0:T(8,128)(2,1)S(1)}, bf16[768,512]{1,0:T(8,128)(2,1)}, u32[]{:S(2)}, u32[]{:S(2)}) collective-permute-start(bf16[768,512]{1,0:T(8,128)(2,1)S(1)} %collective-permute-done.2.across), channel_id=1, source_target_pairs={{0,1},{1,0},{2,3},{3,2},{4,5},{5,4},{6,7},{7,6},{8,9},{9,8},{10,11... | collective-permute-start | bytes 2359304 | tf_op jit(solution)/shard_map/ppermute | solution.py:25
  44.3 0.1 pad_add_fusion.place_ref
  44.5 0.0 collective-permute-done.own_sibling
  44.5 0.0 copy-start.5
  44.5 1.9 %collective-permute-done.6.across_sibling = bf16[768,512]{1,0:T(8,128)(2,1)} collective-permute-done((bf16[768,512]{1,0:T(8,128)(2,1)S(1)}, bf16[768,512]{1,0:T(8,128)(2,1)}, u32[]{:S(2)}, u32[]{:S(2)}) %collective-permute-start.6) | collective-permute-done | bytes 786464 | tf_op jit(solution)/shard_map/ppermute | solution.py:25
  46.4 0.0 copy-done.6
  46.4 0.0 copy-done.5
  46.4 4.6 %shard_map.112 = bf16[16,2,2,64,256]{4,3,2,1,0:T(8,128)(2,1)} custom-call(s32[1]{0:T(128)} %bitcast.core_ref, bf16[768,512]{1,0:T(8,128)(2,1)} %own.1, bf16[768,512]{1,0:T(8,128)(2,1)} %copy-done.5, bf16[768,512]{1,0:T(8,128)(2,1)} %copy-done.4, bf16[768,512]{1,0:T(8,128)(2,1)} %collective-permute-done.6.across_sibling, bf16[768,256]{1,0:T(8,128)(2,1)} %shard_map.111.grads, ...), custom_call_target="tpu_custom_call" | custom-call | flops 2147483648 | bytes 4194304 | tf_op jit(solution)/shard_map/pallas_call | solution.py:128
  51.0 33.4 %all_to_all.15 = bf16[16,4,64,256]{3,2,1,0:T(8,128)(2,1)S(1)} all-to-all(bf16[16,4,64,256]{3,2,1,0:T(8,128)(2,1)} %bitcast.24), channel_id=1, replica_groups=mesh['zh'=4,'zl'=2,'yl'=2,'x'=4,'ya'=2,'yb'=2,'c'=2] {'zl','x','yl'}, dimensions={0} | all-to-all | bytes 4194304 | tf_op jit(solution)/shard_map/all_to_all | solution.py:29
  84.4 0.4 reduce_sum.12
  84.9 27.6 %all_to_all.16 = bf16[8,2,64,256]{3,2,1,0:T(8,128)(2,1)S(1)} all-to-all(bf16[8,2,64,256]{3,2,1,0:T(8,128)(2,1)S(1)} %bitcast.23), channel_id=1, replica_groups=mesh['zh'=4,'zl'=2,'yl'=2,'x'=4,'ya'=2,'yb'=2,'c'=2] {'zh','yb'}, dimensions={0} | all-to-all | bytes 1048576 | tf_op jit(solution)/shard_map/all_to_all | solution.py:29
  112.5 1.4 %shard_map.113 = (f32[64,128]{1,0:T(8,128)}, f32[64,128]{1,0:T(8,128)}, f32[64,128]{1,0:T(8,128)}, bf16[16,4,64,128]{3,2,1,0:T(8,128)(2,1)S(1)}) custom-call(s32[2]{0:T(128)S(1)} %pad_add_fusion.place_ref, bf16[4,2,2,64,256]{4,3,2,1,0:T(8,128)(2,1)S(1)} %bitcast.21, f32[4,3,64,128]{3,2,1,0:T(8,128)S(1)} %pad_maximum_fusion.states_ref), custom_call_target="tpu_custom_call" | custom-call | flops 2097152 | bytes 2097152 | tf_op jit(solution)/shard_map/pallas_call | solution.py:177
  113.9 16.2 %all_to_all.17 = bf16[16,4,64,128]{3,2,1,0:T(8,128)(2,1)S(1)} all-to-all(bf16[16,4,64,128]{3,2,1,0:T(8,128)(2,1)S(1)} %get-tuple-element.33), channel_id=1, replica_groups=mesh['zh'=4,'zl'=2,'yl'=2,'x'=4,'ya'=2,'yb'=2,'c'=2] {'zl','x','yl'}, dimensions={0} | all-to-all | bytes 2097152 | tf_op jit(solution)/shard_map/all_to_all | solution.py:29
  130.1 1.1 copy.12
  (10 shorter events, 0.1 us)
Async XLA Ops:
  0.6 32.1 %copy-start.3 = (bf16[768,512]{1,0:T(8,128)(2,1)S(1)}, bf16[768,512]{1,0:T(8,128)(2,1)}, u32[]{:S(2)}) copy-start(bf16[768,512]{1,0:T(8,128)(2,1)} %own.1) | copy-start | bytes 2359300
  0.6 11.7 %copy-start.2 = (f32[64,128]{1,0:T(8,128)S(1)}, f32[64,128]{1,0:T(8,128)}, u32[]{:S(2)}) copy-start(f32[64,128]{1,0:T(8,128)} %param.13) | copy-start | bytes 98308
  0.7 11.7 %copy-start.1 = (f32[64,128]{1,0:T(8,128)S(1)}, f32[64,128]{1,0:T(8,128)}, u32[]{:S(2)}) copy-start(f32[64,128]{1,0:T(8,128)} %param.14) | copy-start | bytes 98308
  0.7 11.7 %copy-start = (f32[64,128]{1,0:T(8,128)S(1)}, f32[64,128]{1,0:T(8,128)}, u32[]{:S(2)}) copy-start(f32[64,128]{1,0:T(8,128)} %param.15) | copy-start | bytes 98308
  0.7 41.1 %collective-permute-start.2 = (bf16[768,512]{1,0:T(8,128)(2,1)}, bf16[768,512]{1,0:T(8,128)(2,1)S(1)}, u32[]{:S(2)}, u32[]{:S(2)}) collective-permute-start(bf16[768,512]{1,0:T(8,128)(2,1)} %own.1), channel_id=1, source_target_pairs={{0,6},{2,4},{4,2},{6,0},{1,7},{3,5},{5,3},{7,1},{8,14},{10,12},{12... | collective-permute-start | bytes 2359304 | tf_op jit(solution)/shard_map/ppermute | solution.py:25
  12.4 28.1 %collective-permute-start.1 = (bf16[768,256]{1,0:T(8,128)(2,1)}, bf16[768,256]{1,0:T(8,128)(2,1)S(1)}, u32[]{:S(2)}, u32[]{:S(2)}) collective-permute-start(bf16[768,256]{1,0:T(8,128)(2,1)} %shard_map.111.grads), channel_id=1, source_target_pairs={{0,2},{2,0},{1,3},{3,1},{4,6},{6,4},{5,7},{7,5},{8,10},{10,8},{9,1... | collective-permute-start | bytes 1179656 | tf_op jit(solution)/shard_map/ppermute | solution.py:25
  16.2 16.6 %collective-permute-start.3 = (f32[3,64,128]{2,1,0:T(8,128)S(1)}, f32[3,64,128]{2,1,0:T(8,128)S(1)}, u32[]{:S(2)}, u32[]{:S(2)}) collective-permute-start(f32[3,64,128]{2,1,0:T(8,128)S(1)} %pad_maximum_fusion.2), channel_id=1, source_target_pairs={{0,128},{128,0},{256,384},{384,256},{1,129},{129,1},{257,385},{385... | collective-permute-start | bytes 294920 | tf_op jit(solution)/shard_map/ppermute | solution.py:25
  22.0 14.5 %collective-permute-start.4 = (f32[3,64,128]{2,1,0:T(8,128)S(1)}, f32[3,64,128]{2,1,0:T(8,128)S(1)}, u32[]{:S(2)}, u32[]{:S(2)}) collective-permute-start(f32[3,64,128]{2,1,0:T(8,128)S(1)} %pad_maximum_fusion.2), channel_id=1, source_target_pairs={{0,256},{128,384},{256,0},{384,128},{1,257},{129,385},{257,1},{385... | collective-permute-start | bytes 294920 | tf_op jit(solution)/shard_map/ppermute | solution.py:25
  30.8 9.7 %collective-permute-start.5 = (f32[3,64,128]{2,1,0:T(8,128)S(1)}, f32[3,64,128]{2,1,0:T(8,128)S(1)}, u32[]{:S(2)}, u32[]{:S(2)}) collective-permute-start(f32[3,64,128]{2,1,0:T(8,128)S(1)} %pad_maximum_fusion.2), channel_id=1, source_target_pairs={{0,384},{128,256},{256,128},{384,0},{1,385},{129,257},{257,129},{3... | collective-permute-start | bytes 294920 | tf_op jit(solution)/shard_map/ppermute | solution.py:25
  32.8 11.7 %collective-permute-start = (bf16[768,512]{1,0:T(8,128)(2,1)S(1)}, bf16[768,512]{1,0:T(8,128)(2,1)S(1)}, u32[]{:S(2)}, u32[]{:S(2)}) collective-permute-start(bf16[768,512]{1,0:T(8,128)(2,1)S(1)} %copy-done.3), channel_id=1, source_target_pairs={{0,1},{1,0},{2,3},{3,2},{4,5},{5,4},{6,7},{7,6},{8,9},{9,8},{10,11... | collective-permute-start | bytes 2359304 | tf_op jit(solution)/shard_map/ppermute | solution.py:25
  40.5 5.8 %copy-start.6 = (bf16[768,256]{1,0:T(8,128)(2,1)}, bf16[768,256]{1,0:T(8,128)(2,1)S(1)}, u32[]{:S(2)}) copy-start(bf16[768,256]{1,0:T(8,128)(2,1)S(1)} %collective-permute-done.1.other) | copy-start | bytes 1179652
  41.8 4.5 %copy-start.4 = (bf16[768,512]{1,0:T(8,128)(2,1)}, bf16[768,512]{1,0:T(8,128)(2,1)S(1)}, u32[]{:S(2)}) copy-start(bf16[768,512]{1,0:T(8,128)(2,1)S(1)} %collective-permute-done.2.across) | copy-start | bytes 2359300
  41.8 4.5 %collective-permute-start.6 = (bf16[768,512]{1,0:T(8,128)(2,1)S(1)}, bf16[768,512]{1,0:T(8,128)(2,1)}, u32[]{:S(2)}, u32[]{:S(2)}) collective-permute-start(bf16[768,512]{1,0:T(8,128)(2,1)S(1)} %collective-permute-done.2.across), channel_id=1, source_target_pairs={{0,1},{1,0},{2,3},{3,2},{4,5},{5,4},{6,7},{7,6},{8,9},{9,8},{10,11... | collective-permute-start | bytes 2359304 | tf_op jit(solution)/shard_map/ppermute | solution.py:25
  44.5 1.9 %copy-start.5 = (bf16[768,512]{1,0:T(8,128)(2,1)}, bf16[768,512]{1,0:T(8,128)(2,1)S(1)}, u32[]{:S(2)}) copy-start(bf16[768,512]{1,0:T(8,128)(2,1)S(1)} %collective-permute-done.own_sibling) | copy-start | bytes 2359300

commit v5 on v3

--- a/solution.py
+++ b/solution.py
@@ -136,10 +136,10 @@
     rows, width = master.shape
     pair = 2 * width
     across = swap(activations, ("ya", "yb"), 4, 3)
-    sibling = swap(activations, "c", 2, 1)
     own = attention_grads(query_rows, key_rows, true_cotangent, sample_cotangent)
     state = jnp.stack((master, moment, curvature))
-    own, state = lax.optimization_barrier((own, state))
+    own, state, halves = lax.optimization_barrier((own, state, activations))
+    sibling = swap(halves, "c", 2, 1)
     other = swap(own, "yb", 2, 1)
     moved = tuple(swap(state, "zh", 4, flip) for flip in (1, 2, 3))
     other, across, moved = lax.optimization_barrier((other, across, moved))
@@ -170,8 +170,9 @@
     part = jnp.broadcast_to(part[None], (4, 2, 2, rows, pair)).reshape(8, 2, rows, pair)
     part = exchange(part, ("zh", "yb"))
     *ours, weights = update(place, part.reshape(4, 2, 2, rows, pair), states)
-    weights = exchange(weights, NEAR)
-    weights_next = weights.transpose(1, 0, 2, 3).reshape(64 * rows, width)
+    weights = exchange(weights, ("zl", "x", "yl"))
+    weights_next = weights.reshape(2, 4, 2, 4, rows, width).transpose(3, 0, 2, 1, 4, 5)
+    weights_next = weights_next.reshape(64 * rows, width)
     return (*ours, weights_next)
 
 

time: 135 us -> 134 us (level)
  blocking collectives: 81.5 us -> 79.9 us
    all_to_all x3, blocking collectives: 81.5 us -> 79.9 us  [exchange(): return lax.all_to_all(v, axes, 0, 0, tiled=True)]
where the time goes in v5:
time: 134 us; the launch traced here: 133 us
  blocking collectives  79.9 us (60%)
  starting transfers between devices  34.7 us (26%)
  waiting for transfers between devices  6.65 us (5%)
  Pallas kernels  6.22 us (5%)
  matrix products  2.49 us (2%)
  local copies, waits for them, and re-layouts  1.49 us (1%)
    all_to_all x3, blocking collectives, exchange(): return lax.all_to_all(v, axes, 0, 0, tiled=True)  79.9 us
    ppermute x7, starting transfers between devices, swap(): return lax.ppermute(v, axes, [(i, i ^ flip) for i in range(size)])  34.7 us
    ppermute x7, waiting for transfers between devices, swap(): return lax.ppermute(v, axes, [(i, i ^ flip) for i in range(size)])  6.65 us
    pallas_call x1, Pallas kernels, attention_grads(): pl.pallas_call(attention_kernel, in_specs=[whole] * 4, out_specs=whole, o...  4.83 us
  transfers between devices with their start and end apart: 7, of which 3 were waited for; matrix products, arithmetic and copies ran while one was open for 1% of the time, Pallas kernels for 4%

profile of v5, /device:TPU:1, one launch (start us, length us, event | category | flops | bytes accessed | tf_op | source)
XLA Modules:
  0.0 133.4 jit_solution(6253436471342026199)
XLA Ops:
  0.7 6.8 %collective-permute-start.2 = (bf16[768,512]{1,0:T(8,128)(2,1)}, bf16[768,512]{1,0:T(8,128)(2,1)S(1)}, u32[]{:S(2)}, u32[]{:S(2)}) collective-permute-start(bf16[768,512]{1,0:T(8,128)(2,1)} %param.8), channel_id=1, source_target_pairs={{0,6},{2,4},{4,2},{6,0},{1,7},{3,5},{5,3},{7,1},{8,14},{10,12},{12... | collective-permute-start | bytes 2359304 | tf_op jit(solution)/shard_map/ppermute | solution.py:25
  7.5 4.8 %shard_map.111 = bf16[768,256]{1,0:T(8,128)(2,1)} custom-call(bf16[768,512]{1,0:T(8,128)(2,1)} %query_ref.1, bf16[768,128]{1,0:T(8,128)(2,1)} %key_ref.1, bf16[768,512]{1,0:T(8,128)(2,1)} %true_ref.1, bf16[768,512]{1,0:T(8,128)(2,1)} %sample_ref.1), custom_call_target="tpu_custom_call" | custom-call | tf_op jit(solution)/shard_map/pallas_call | solution.py:78
  12.4 4.1 %collective-permute-start = (bf16[768,512]{1,0:T(8,128)(2,1)S(1)}, bf16[768,512]{1,0:T(8,128)(2,1)S(1)}, u32[]{:S(2)}, u32[]{:S(2)}) collective-permute-start(bf16[768,512]{1,0:T(8,128)(2,1)S(1)} %copy-done), channel_id=1, source_target_pairs={{0,1},{1,0},{2,3},{3,2},{4,5},{5,4},{6,7},{7,6},{8,9},{9,8},{10,11... | collective-permute-start | bytes 2359304 | tf_op jit(solution)/shard_map/ppermute | solution.py:25
  16.5 2.6 %collective-permute-start.1 = (bf16[768,256]{1,0:T(8,128)(2,1)}, bf16[768,256]{1,0:T(8,128)(2,1)S(1)}, u32[]{:S(2)}, u32[]{:S(2)}) collective-permute-start(bf16[768,256]{1,0:T(8,128)(2,1)} %shard_map.111), channel_id=1, source_target_pairs={{0,2},{2,0},{1,3},{3,1},{4,6},{6,4},{5,7},{7,5},{8,10},{10,8},{9,1... | collective-permute-start | bytes 1179656 | tf_op jit(solution)/shard_map/ppermute | solution.py:25
  19.2 5.8 %collective-permute-start.3 = (f32[3,64,128]{2,1,0:T(8,128)S(1)}, f32[3,64,128]{2,1,0:T(8,128)S(1)}, u32[]{:S(2)}, u32[]{:S(2)}) collective-permute-start(f32[3,64,128]{2,1,0:T(8,128)S(1)} %pad_maximum_fusion.9), channel_id=1, source_target_pairs={{0,128},{128,0},{256,384},{384,256},{1,129},{129,1},{257,385},{385... | collective-permute-start | bytes 294920 | tf_op jit(solution)/shard_map/ppermute | solution.py:25
  25.0 8.8 %collective-permute-start.4 = (f32[3,64,128]{2,1,0:T(8,128)S(1)}, f32[3,64,128]{2,1,0:T(8,128)S(1)}, u32[]{:S(2)}, u32[]{:S(2)}) collective-permute-start(f32[3,64,128]{2,1,0:T(8,128)S(1)} %pad_maximum_fusion.9), channel_id=1, source_target_pairs={{0,256},{128,384},{256,0},{384,128},{1,257},{129,385},{257,1},{385... | collective-permute-start | bytes 294920 | tf_op jit(solution)/shard_map/ppermute | solution.py:25
  33.8 0.0 collective-permute-done.3
  33.9 4.1 %collective-permute-start.5 = (f32[3,64,128]{2,1,0:T(8,128)S(1)}, f32[3,64,128]{2,1,0:T(8,128)S(1)}, u32[]{:S(2)}, u32[]{:S(2)}) collective-permute-start(f32[3,64,128]{2,1,0:T(8,128)S(1)} %pad_maximum_fusion.9), channel_id=1, source_target_pairs={{0,384},{128,256},{256,128},{384,0},{1,385},{129,257},{257,129},{3... | collective-permute-start | bytes 294920 | tf_op jit(solution)/shard_map/ppermute | solution.py:25
  38.0 0.1 pad_add_fusion.place_ref
  38.1 0.0 collective-permute-done.4
  38.1 5.2 %collective-permute-done.5 = f32[3,64,128]{2,1,0:T(8,128)S(1)} collective-permute-done((f32[3,64,128]{2,1,0:T(8,128)S(1)}, f32[3,64,128]{2,1,0:T(8,128)S(1)}, u32[]{:S(2)}, u32[]{:S(2)}) %collective-permute-start.5) | collective-permute-done | bytes 98336 | tf_op jit(solution)/shard_map/ppermute | solution.py:25
  43.2 1.4 %collective-permute-done.1 = bf16[768,256]{1,0:T(8,128)(2,1)S(1)} collective-permute-done((bf16[768,256]{1,0:T(8,128)(2,1)}, bf16[768,256]{1,0:T(8,128)(2,1)S(1)}, u32[]{:S(2)}, u32[]{:S(2)}) %collective-permute-start.1) | collective-permute-done | bytes 393248 | tf_op jit(solution)/shard_map/ppermute | solution.py:25
  44.6 0.0 collective-permute-done.2
  44.6 2.3 %collective-permute-start.6 = (bf16[768,512]{1,0:T(8,128)(2,1)S(1)}, bf16[768,512]{1,0:T(8,128)(2,1)S(1)}, u32[]{:S(2)}, u32[]{:S(2)}) collective-permute-start(bf16[768,512]{1,0:T(8,128)(2,1)S(1)} %collective-permute-done.2), channel_id=1, source_target_pairs={{0,1},{1,0},{2,3},{3,2},{4,5},{5,4},{6,7},{7,6},{8,9},{9,8},{10,11... | collective-permute-start | bytes 2359304 | tf_op jit(solution)/shard_map/ppermute | solution.py:25
  47.0 0.0 copy-done.5
  47.0 0.0 collective-permute-done
  47.0 0.1 broadcast_select_fusion.3
  47.2 0.0 copy-done.1
  47.2 0.6 convolution_convert_fusion.3
  47.8 0.4 copy-done.6
  48.2 0.6 convolution_convert_fusion.1
  48.8 0.1 collective-permute-done.6
  48.9 0.1 broadcast_select_fusion.1
  49.0 0.6 convolution_convert_fusion.2
  49.6 0.6 convolution_convert_fusion
  50.2 0.3 pad_maximum_fusion
  50.5 34.8 %all_to_all.15 = bf16[16,4,64,256]{3,2,1,0:T(8,128)(2,1)S(1)} all-to-all(bf16[16,4,64,256]{3,2,1,0:T(8,128)(2,1)S(1)} %pad_maximum_fusion), channel_id=1, replica_groups=mesh['zh'=4,'zl'=2,'yl'=2,'x'=4,'ya'=2,'yb'=2,'c'=2] {'zl','yl','x'}, dimensions={0} | all-to-all | bytes 4194304 | tf_op jit(solution)/shard_map/all_to_all | solution.py:29
  85.3 0.4 reduce_sum.12
  85.8 28.2 %all_to_all.16 = bf16[8,2,64,256]{3,2,1,0:T(8,128)(2,1)S(1)} all-to-all(bf16[8,2,64,256]{3,2,1,0:T(8,128)(2,1)S(1)} %bitcast.37), channel_id=1, replica_groups=mesh['zh'=4,'zl'=2,'yl'=2,'x'=4,'ya'=2,'yb'=2,'c'=2] {'zh','yb'}, dimensions={0} | all-to-all | bytes 1048576 | tf_op jit(solution)/shard_map/all_to_all | solution.py:29
  114.0 1.4 %shard_map.112 = (f32[64,128]{1,0:T(8,128)}, f32[64,128]{1,0:T(8,128)}, f32[64,128]{1,0:T(8,128)}, bf16[16,4,64,128]{3,2,1,0:T(8,128)(2,1)S(1)}) custom-call(s32[2]{0:T(128)S(1)} %pad_add_fusion.place_ref, bf16[4,2,2,64,256]{4,3,2,1,0:T(8,128)(2,1)S(1)} %bitcast.35, f32[4,3,64,128]{3,2,1,0:T(8,128)S(1)} %pad_maximum_fusion.7.states_ref), custom_call_target="tpu_custom_call" | custom-call | flops 2097152 | bytes 2097152 | tf_op jit(solution)/shard_map/pallas_call | solution.py:121
  115.4 17.0 %all_to_all.17 = bf16[16,4,64,128]{3,2,1,0:T(8,128)(2,1)S(1)} all-to-all(bf16[16,4,64,128]{3,2,1,0:T(8,128)(2,1)S(1)} %get-tuple-element.35), channel_id=1, replica_groups=mesh['zh'=4,'zl'=2,'yl'=2,'x'=4,'ya'=2,'yb'=2,'c'=2] {'zl','x','yl'}, dimensions={0} | all-to-all | bytes 2097152 | tf_op jit(solution)/shard_map/all_to_all | solution.py:29
  132.3 1.1 copy.17
  (16 shorter events, 0.1 us)
Async XLA Ops:
  0.6 11.8 %copy-start = (bf16[768,512]{1,0:T(8,128)(2,1)S(1)}, bf16[768,512]{1,0:T(8,128)(2,1)}, u32[]{:S(2)}) copy-start(bf16[768,512]{1,0:T(8,128)(2,1)} %param.8) | copy-start | bytes 2359300
  0.6 11.7 %copy-start.4 = (f32[64,128]{1,0:T(8,128)S(1)}, f32[64,128]{1,0:T(8,128)}, u32[]{:S(2)}) copy-start(f32[64,128]{1,0:T(8,128)} %param.13) | copy-start | bytes 98308
  0.7 11.7 %copy-start.3 = (f32[64,128]{1,0:T(8,128)S(1)}, f32[64,128]{1,0:T(8,128)}, u32[]{:S(2)}) copy-start(f32[64,128]{1,0:T(8,128)} %param.14) | copy-start | bytes 98308
  0.7 11.7 %copy-start.2 = (f32[64,128]{1,0:T(8,128)S(1)}, f32[64,128]{1,0:T(8,128)}, u32[]{:S(2)}) copy-start(f32[64,128]{1,0:T(8,128)} %param.15) | copy-start | bytes 98308
  0.7 44.0 %collective-permute-start.2 = (bf16[768,512]{1,0:T(8,128)(2,1)}, bf16[768,512]{1,0:T(8,128)(2,1)S(1)}, u32[]{:S(2)}, u32[]{:S(2)}) collective-permute-start(bf16[768,512]{1,0:T(8,128)(2,1)} %param.8), channel_id=1, source_target_pairs={{0,6},{2,4},{4,2},{6,0},{1,7},{3,5},{5,3},{7,1},{8,14},{10,12},{12... | collective-permute-start | bytes 2359304 | tf_op jit(solution)/shard_map/ppermute | solution.py:25
  12.4 34.8 %copy-start.1 = (bf16[768,256]{1,0:T(8,128)(2,1)S(1)}, bf16[768,256]{1,0:T(8,128)(2,1)}, u32[]{:S(2)}) copy-start(bf16[768,256]{1,0:T(8,128)(2,1)} %shard_map.111) | copy-start | bytes 1179652
  12.4 34.6 %collective-permute-start = (bf16[768,512]{1,0:T(8,128)(2,1)S(1)}, bf16[768,512]{1,0:T(8,128)(2,1)S(1)}, u32[]{:S(2)}, u32[]{:S(2)}) collective-permute-start(bf16[768,512]{1,0:T(8,128)(2,1)S(1)} %copy-done), channel_id=1, source_target_pairs={{0,1},{1,0},{2,3},{3,2},{4,5},{5,4},{6,7},{7,6},{8,9},{9,8},{10,11... | collective-permute-start | bytes 2359304 | tf_op jit(solution)/shard_map/ppermute | solution.py:25
  16.5 28.1 %collective-permute-start.1 = (bf16[768,256]{1,0:T(8,128)(2,1)}, bf16[768,256]{1,0:T(8,128)(2,1)S(1)}, u32[]{:S(2)}, u32[]{:S(2)}) collective-permute-start(bf16[768,256]{1,0:T(8,128)(2,1)} %shard_map.111), channel_id=1, source_target_pairs={{0,2},{2,0},{1,3},{3,1},{4,6},{6,4},{5,7},{7,5},{8,10},{10,8},{9,1... | collective-permute-start | bytes 1179656 | tf_op jit(solution)/shard_map/ppermute | solution.py:25
  19.2 14.7 %collective-permute-start.3 = (f32[3,64,128]{2,1,0:T(8,128)S(1)}, f32[3,64,128]{2,1,0:T(8,128)S(1)}, u32[]{:S(2)}, u32[]{:S(2)}) collective-permute-start(f32[3,64,128]{2,1,0:T(8,128)S(1)} %pad_maximum_fusion.9), channel_id=1, source_target_pairs={{0,128},{128,0},{256,384},{384,256},{1,129},{129,1},{257,385},{385... | collective-permute-start | bytes 294920 | tf_op jit(solution)/shard_map/ppermute | solution.py:25
  25.0 13.1 %collective-permute-start.4 = (f32[3,64,128]{2,1,0:T(8,128)S(1)}, f32[3,64,128]{2,1,0:T(8,128)S(1)}, u32[]{:S(2)}, u32[]{:S(2)}) collective-permute-start(f32[3,64,128]{2,1,0:T(8,128)S(1)} %pad_maximum_fusion.9), channel_id=1, source_target_pairs={{0,256},{128,384},{256,0},{384,128},{1,257},{129,385},{257,1},{385... | collective-permute-start | bytes 294920 | tf_op jit(solution)/shard_map/ppermute | solution.py:25
  33.9 9.4 %collective-permute-start.5 = (f32[3,64,128]{2,1,0:T(8,128)S(1)}, f32[3,64,128]{2,1,0:T(8,128)S(1)}, u32[]{:S(2)}, u32[]{:S(2)}) collective-permute-start(f32[3,64,128]{2,1,0:T(8,128)S(1)} %pad_maximum_fusion.9), channel_id=1, source_target_pairs={{0,384},{128,256},{256,128},{384,0},{1,385},{129,257},{257,129},{3... | collective-permute-start | bytes 294920 | tf_op jit(solution)/shard_map/ppermute | solution.py:25
  44.6 2.4 %copy-start.5 = (bf16[768,256]{1,0:T(8,128)(2,1)}, bf16[768,256]{1,0:T(8,128)(2,1)S(1)}, u32[]{:S(2)}) copy-start(bf16[768,256]{1,0:T(8,128)(2,1)S(1)} %collective-permute-done.1) | copy-start | bytes 1179652
  44.6 4.2 %collective-permute-start.6 = (bf16[768,512]{1,0:T(8,128)(2,1)S(1)}, bf16[768,512]{1,0:T(8,128)(2,1)S(1)}, u32[]{:S(2)}, u32[]{:S(2)}) collective-permute-start(bf16[768,512]{1,0:T(8,128)(2,1)S(1)} %collective-permute-done.2), channel_id=1, source_target_pairs={{0,1},{1,0},{2,3},{3,2},{4,5},{5,4},{6,7},{7,6},{8,9},{9,8},{10,11... | collective-permute-start | bytes 2359304 | tf_op jit(solution)/shard_map/ppermute | solution.py:25
  47.2 1.0 copy-start.6
